TPU v7x, 256 devices: a whole 4x4x8 slice. The times are simulated.
256 devices in a mesh: dom: 32 (over y, z), esplit: 8 (over x, core).
Axes of the slice: x: 4, y: 4, z: 8, core: 2. Of those that a mesh axis runs over, the one named last changes fastest.
Arguments:
- node_state: bfloat16 [32768, 512], P(('dom', 'esplit')), may hold values from -6 to 6
- edge_state: bfloat16 [131072, 512], P(('dom', 'esplit')), may hold values from -6 to 6
- senders: int32 [131072], P(('dom', 'esplit')), may hold values from 0 to 1535
- receivers: int32 [131072], P(('dom', 'esplit')), may hold values from 0 to 1023
- send_rows: int32 [32, 32, 16], P('dom'), may hold values from 0 to 1023
- edge_in: bfloat16 [1, 3, 512, 512], replicated, may hold values from -0.15625 to 0.15625
- edge_out: bfloat16 [1, 512, 512], replicated, may hold values from -0.25 to 0.25
- edge_gain: float32 [1, 512], replicated, may hold values from 0.1 to 1.9
- node_in: bfloat16 [1, 2, 512, 512], replicated, may hold values from -0.1875 to 0.1875
- node_out: bfloat16 [1, 512, 512], replicated, may hold values from -0.25 to 0.25
- node_gain: float32 [1, 512], replicated, may hold values from 0.1 to 1.9
- node_cot: bfloat16 [32768, 512], P(('dom', 'esplit')), may hold values from -6 to 6
- edge_cot: bfloat16 [131072, 512], P(('dom', 'esplit')), may hold values from -24 to 24
Outputs:
- nodes_out: bfloat16 [32768, 512], P(('dom', 'esplit'))
- edges_out: bfloat16 [131072, 512], P(('dom', 'esplit'))
- node_grad: bfloat16 [32768, 512], P(('dom', 'esplit'))
- edge_grad: bfloat16 [131072, 512], P(('dom', 'esplit'))
- weight_grads: float32 [1, 1835008], P(None, ('dom', 'esplit'))
Inputs may be any that keep to these rules, and one draw needn't show every extreme that they name: An edge of partition d sends from row senders of table_d: below 1024 a node of partition d, else ghost slot k from partition p at 1024 + p * 16 + k. `receivers`: A node of the edge's own partition. send_rows[p, d, k] is a node of partition p that fills ghost slot k of partition d; lists are padded, so rows may repeat.
All inputs are finite; a program needn't handle non-finite values.
Results may differ from a plain program's by a relative error of at most 0.018.
Values may be sent and summed in bfloat16 or wider, within the bound.
A program may use at most 128 MiB of HBM per device.

v0:
```python
import jax
import jax.numpy as jnp
from jax import lax
from jax.sharding import PartitionSpec as P

EPSILON = 1e-05


def normalize(values, gain):
    average = jnp.mean(values, axis=-1, keepdims=True)
    centered = values - average
    inv_scale = lax.rsqrt(jnp.mean(centered * centered, axis=-1, keepdims=True) + EPSILON)
    return gain * centered * inv_scale


def normalize_back(values, gain, upstream):
    average = jnp.mean(values, axis=-1, keepdims=True)
    centered = values - average
    inv_scale = lax.rsqrt(jnp.mean(centered * centered, axis=-1, keepdims=True) + EPSILON)
    scaled = centered * inv_scale
    grad_scaled = upstream * gain
    first = jnp.mean(grad_scaled, axis=-1, keepdims=True)
    second = jnp.mean(grad_scaled * scaled, axis=-1, keepdims=True)
    return inv_scale * (grad_scaled - first - scaled * second)


def swish_slope(values):
    sigma = jax.nn.sigmoid(values)
    return sigma * (1.0 + values * (1.0 - sigma))


def outer_sum(left, right):
    return lax.dot_general(
        left, right, (((0,), (0,)), ((), ())), preferred_element_type=jnp.float32
    )


def project_back(grad, weight):
    return lax.dot_general(
        grad, weight, (((1,), (1,)), ((), ())), preferred_element_type=jnp.float32
    )


def edge_forward(edges, sent_rows, recv_rows, w_in, w_out, gain):
    pre_act = jnp.dot(edges, w_in[0], preferred_element_type=jnp.float32)
    pre_act = pre_act + jnp.dot(sent_rows, w_in[1], preferred_element_type=jnp.float32)
    pre_act = pre_act + jnp.dot(recv_rows, w_in[2], preferred_element_type=jnp.float32)
    hidden = jax.nn.silu(pre_act).astype(jnp.bfloat16)
    message = jnp.dot(hidden, w_out, preferred_element_type=jnp.float32)
    updated = (edges.astype(jnp.float32) + normalize(message, gain)).astype(jnp.bfloat16)
    return (updated, pre_act, message, hidden)


def edge_backward(
    edges, sent_rows, recv_rows, pre_act, message, hidden, w_in, w_out, gain, upstream
):
    grad_message = normalize_back(message, gain, upstream).astype(jnp.bfloat16)
    grad_out = outer_sum(hidden, grad_message)
    grad_pre = (project_back(grad_message, w_out) * swish_slope(pre_act)).astype(jnp.bfloat16)
    grad_in = jnp.stack(
        [outer_sum(edges, grad_pre), outer_sum(sent_rows, grad_pre), outer_sum(recv_rows, grad_pre)]
    )
    grad_edges = upstream + project_back(grad_pre, w_in[0])
    return (
        grad_edges,
        project_back(grad_pre, w_in[1]),
        project_back(grad_pre, w_in[2]),
        grad_in,
        grad_out,
    )


def node_forward(nodes, aggregate, w_in, w_out, gain):
    pre_act = jnp.dot(nodes, w_in[0], preferred_element_type=jnp.float32)
    pre_act = pre_act + jnp.dot(aggregate, w_in[1], preferred_element_type=jnp.float32)
    hidden = jax.nn.silu(pre_act).astype(jnp.bfloat16)
    message = jnp.dot(hidden, w_out, preferred_element_type=jnp.float32)
    updated = (nodes.astype(jnp.float32) + normalize(message, gain)).astype(jnp.bfloat16)
    return (updated, pre_act, message, hidden)


def node_backward(nodes, aggregate, pre_act, message, hidden, w_in, w_out, gain, upstream):
    grad_message = normalize_back(message, gain, upstream).astype(jnp.bfloat16)
    grad_out = outer_sum(hidden, grad_message)
    grad_pre = (project_back(grad_message, w_out) * swish_slope(pre_act)).astype(jnp.bfloat16)
    grad_in = jnp.stack([outer_sum(nodes, grad_pre), outer_sum(aggregate, grad_pre)])
    grad_nodes = upstream + project_back(grad_pre, w_in[0])
    grad_aggregate = project_back(grad_pre, w_in[1]).astype(jnp.bfloat16)
    return (grad_nodes, grad_aggregate, grad_in, grad_out)


def body(
    node_state,
    edge_state,
    senders,
    receivers,
    send_rows,
    edge_in,
    edge_out,
    edge_gain,
    node_in,
    node_out,
    node_gain,
    node_cot,
    edge_cot,
):
    lists = send_rows[0]
    peers, ghost = lists.shape
    width = node_state.shape[1]
    splits = lax.axis_size("esplit")
    part_rows = node_state.shape[0] * splits
    table_rows = part_rows + peers * ghost
    layers = edge_in.shape[0]
    layer = 0
    gathered = lax.all_gather(node_state, "esplit", axis=0, tiled=True)
    arrived = lax.all_to_all(gathered[lists], "dom", split_axis=0, concat_axis=0, tiled=True)
    table = jnp.concatenate([gathered, arrived.reshape(peers * ghost, width)])
    sent_rows = table[senders]
    recv_rows = gathered[receivers]
    new_edges, pre_act, message, hidden = edge_forward(
        edge_state, sent_rows, recv_rows, edge_in[layer], edge_out[layer], edge_gain[layer]
    )
    partial_sum = jax.ops.segment_sum(
        new_edges.astype(jnp.float32), receivers, num_segments=part_rows
    )
    aggregate = lax.psum_scatter(partial_sum, "esplit", scatter_dimension=0, tiled=True).astype(
        jnp.bfloat16
    )
    new_nodes, npre, nmsg, nhid = node_forward(
        node_state, aggregate, node_in[layer], node_out[layer], node_gain[layer]
    )
    saved = [
        (
            node_state,
            edge_state,
            sent_rows,
            recv_rows,
            pre_act,
            message,
            hidden,
            aggregate,
            npre,
            nmsg,
            nhid,
        )
    ]
    grad_nodes = node_cot.astype(jnp.float32)
    grad_edges = edge_cot.astype(jnp.float32)
    flats = []
    for layer in reversed(range(layers)):
        (
            old_nodes,
            old_edges,
            sent_rows,
            recv_rows,
            pre_act,
            message,
            hidden,
            aggregate,
            npre,
            nmsg,
            nhid,
        ) = saved[layer]
        direct, grad_agg, gn_in, gn_out = node_backward(
            old_nodes,
            aggregate,
            npre,
            nmsg,
            nhid,
            node_in[layer],
            node_out[layer],
            node_gain[layer],
            grad_nodes,
        )
        agg_full = lax.all_gather(grad_agg, "esplit", axis=0, tiled=True)
        total = grad_edges + agg_full[receivers].astype(jnp.float32)
        grad_edges, grad_sent, grad_recv, ge_in, ge_out = edge_backward(
            old_edges,
            sent_rows,
            recv_rows,
            pre_act,
            message,
            hidden,
            edge_in[layer],
            edge_out[layer],
            edge_gain[layer],
            total,
        )
        dtable = jax.ops.segment_sum(
            jnp.concatenate([grad_sent, grad_recv]),
            jnp.concatenate([senders, receivers]),
            num_segments=table_rows,
        )
        local_grad = dtable[:part_rows]
        ghost_grad = dtable[part_rows:].reshape(peers, ghost, width)
        returned = lax.all_to_all(
            ghost_grad.astype(jnp.bfloat16), "dom", split_axis=0, concat_axis=0, tiled=True
        ).astype(ghost_grad.dtype)
        local_grad = local_grad + jax.ops.segment_sum(
            returned.reshape(peers * ghost, width), lists.reshape(-1), num_segments=part_rows
        )
        grad_nodes = direct + lax.psum_scatter(
            local_grad.astype(jnp.bfloat16), "esplit", scatter_dimension=0, tiled=True
        ).astype(jnp.float32)
        flat = jnp.concatenate(
            [ge_in.reshape(-1), ge_out.reshape(-1), gn_in.reshape(-1), gn_out.reshape(-1)]
        )
        flats.insert(0, flat)
    weight_grads = lax.psum_scatter(
        jnp.stack(flats), ("dom", "esplit"), scatter_dimension=1, tiled=True
    )
    return (
        new_nodes,
        new_edges,
        grad_nodes.astype(jnp.bfloat16),
        grad_edges.astype(jnp.bfloat16),
        weight_grads,
    )


def solution(mesh):
    in_specs = (
        P(("dom", "esplit"), None),
        P(("dom", "esplit"), None),
        P(("dom", "esplit")),
        P(("dom", "esplit")),
        P("dom", None, None),
        P(),
        P(),
        P(),
        P(),
        P(),
        P(),
        P(("dom", "esplit"), None),
        P(("dom", "esplit"), None),
    )
    out_specs = (
        P(("dom", "esplit"), None),
        P(("dom", "esplit"), None),
        P(("dom", "esplit"), None),
        P(("dom", "esplit"), None),
        P(None, ("dom", "esplit")),
    )
    return jax.shard_map(body, mesh=mesh, in_specs=in_specs, out_specs=out_specs, check_vma=False)
```

profile of v0, /device:TPU:14, one launch (start us, length us, event | category | flops | bytes accessed | tf_op | source)
XLA Modules:
  0.0 523.1 jit_solution(12315593927089394902)
XLA Ops:
  8.8 28.1 %all-gather.3.cloned.1.call-done = bf16[1024,512]{1,0:T(8,128)(2,1)} async-done(((bf16[128,512]{1,0:T(8,128)(2,1)}), bf16[1024,512]{1,0:T(8,128)(2,1)}) %all-gather.3.cloned.1.call-update) | async-done | bytes 1048592 | tf_op jit(solution)/shard_map/all_gather | solution.py:115
  36.9 4.0 gather_fusion
  41.0 10.3 %all-to-all-start = ((bf16[32,16,512]{2,1,0:T(8,128)(2,1)}), bf16[32,16,512]{2,1,0:T(8,128)(2,1)S(1)}, u32[]{:S(2)}, u32[]{:S(2)}) async-start(bf16[32,16,512]{2,1,0:T(8,128)(2,1)} %bitcast.5), calls=%async_computation | async-start | bytes 1048576 | tf_op jit(solution)/shard_map/all_to_all | solution.py:116
  52.4 2.5 fusion.31
  54.9 2.6 gather_fusion.2
  57.5 9.7 %all-to-all-done = bf16[32,16,512]{2,1,0:T(8,128)(2,1)S(1)} async-done(((bf16[32,16,512]{2,1,0:T(8,128)(2,1)}), bf16[32,16,512]{2,1,0:T(8,128)(2,1)S(1)}, u32[]{:S(2)}, u32[]{:S(2)}) %all-to-all-start) | async-done | bytes 524320 | tf_op jit(solution)/shard_map/all_to_all | solution.py:116
  69.2 2.0 gather_fusion.1
  71.2 2.0 convolution_add_fusion.2
  73.2 1.5 convolution_add_fusion.1
  77.9 5.7 %scatter_custom_fusion = f32[1024,512]{1,0:T(8,128)} fusion(s32[512]{0:T(512)S(1)} %copy-done.37, f32[512,512]{1,0:T(8,128)} %copy.43, f32[]{:T(128)} %constant.10.clone.1), kind=kCustom, calls=%fused_computation.46 | custom fusion | flops 262144 | bytes 2097664 | tf_op jit(solution)/shard_map/scatter-add | solution.py:123
  85.2 29.8 %reduce-scatter.4.cloned.1.call-done = f32[128,512]{1,0:T(8,128)} async-done(((f32[1024,512]{1,0:T(8,128)}), f32[128,512]{1,0:T(8,128)}) %reduce-scatter.4.cloned.1.call-update) | async-done | bytes 262160 | tf_op jit(solution)/shard_map/reduce_scatter | solution.py:126
  115.0 1.4 convolution_add_fusion.4
  116.4 1.4 fusion.58
  126.2 1.5 pad_maximum_fusion.2
  127.7 2.9 copy.52
  130.6 3.5 copy.63
  134.1 12.8 %all-gather.5.cloned.1.call-done = bf16[1024,512]{1,0:T(8,128)(2,1)} async-done(((bf16[128,512]{1,0:T(8,128)(2,1)}), bf16[1024,512]{1,0:T(8,128)(2,1)}) %all-gather.5.cloned.1.call-update) | async-done | bytes 1048592 | tf_op jit(solution)/shard_map/all_gather | solution.py:175
  146.9 4.0 gather_fusion.3
  155.6 1.4 fusion.27
  157.1 9.3 %scatter_custom_fusion.1 = f32[1536,512]{1,0:T(8,128)} fusion(s32[1024]{0:T(1024)S(1)} %pad_add_fusion, f32[512,512]{1,0:T(8,128)S(1)} %fusion.24, f32[]{:T(128)} %constant.39, f32[512,512]{1,0:T(8,128)} %fusion.27, f32[]{:T(128)} %constant.10.clone.1), kind=kCustom, calls=%fused_computation.9 | custom fusion | flops 1048576 | bytes 5242888 | tf_op jit(solution)/shard_map/scatter-add | solution.py:189
  166.4 1.9 copy-done.3
  169.1 10.2 %all-to-all-start.1 = ((bf16[32,16,512]{2,1,0:T(8,128)(2,1)}), bf16[32,16,512]{2,1,0:T(8,128)(2,1)}, u32[]{:S(2)}, u32[]{:S(2)}) async-start(bf16[32,16,512]{2,1,0:T(8,128)(2,1)} %bitcast.12), calls=%async_computation.2 | async-start | bytes 1048576 | tf_op jit(solution)/shard_map/all_to_all | solution.py:196
  182.9 2.0 pad_maximum_fusion.1
  184.9 3.5 copy.50
  188.5 4.6 copy.61
  193.1 2.3 all-to-all-done.1
  195.4 4.9 scatter_custom_fusion.2
  201.5 7.7 %pad_maximum_fusion = f32[1835008]{0:T(1024)} fusion(f32[262144]{0:T(1024)} %bitcast.102, f32[524288]{0:T(1024)} %bitcast.100, f32[262144]{0:T(1024)} %bitcast.103, f32[786432]{0:T(1024)} %bitcast.98), kind=kLoop, calls=%fused_computation.7 | loop fusion | flops 5505024 | bytes 14680064 | tf_op jit(solution)/shard_map/concatenate | solution.py:205
  211.3 1.6 fusion.6
  213.9 17.9 %reduce-scatter.6.cloned.1.call-done = bf16[128,512]{1,0:T(8,128)(2,1)} async-done(((bf16[1024,512]{1,0:T(8,128)(2,1)}), bf16[128,512]{1,0:T(8,128)(2,1)}) %reduce-scatter.6.cloned.1.call-update) | async-done | bytes 131088 | tf_op jit(solution)/shard_map/reduce_scatter | solution.py:202
  231.8 2.0 fusion.9
  233.8 281.4 %all-reduce.3.cloned.1.call-done = f32[1,1835008]{1,0:T(1,128)} async-done(((f32[1,1835008]{1,0:T(1,128)}), f32[1,1835008]{1,0:T(1,128)}) %all-reduce.3.cloned.1.call-update) | async-done | bytes 7340048
  (150 shorter events, 32.1 us)
Async XLA Ops:
  7.2 67.5 %copy-start = (bf16[1,512,512]{2,1,0:T(8,128)(2,1)S(1)}, bf16[1,512,512]{2,1,0:T(8,128)(2,1)}, u32[]{:S(2)}) copy-start(bf16[1,512,512]{2,1,0:T(8,128)(2,1)} %param.19) | copy-start | bytes 1572868
  7.2 29.8 %all-gather.3.cloned.1.call-start = ((), (), s32[]{:S(2)}) async-start(), calls=%async_computation.4 | async-start | bytes 1179648 | tf_op jit(solution)/shard_map/all_gather | solution.py:115
  8.8 42.5 %copy-start.13 = (bf16[512,512]{1,0:T(8,128)(2,1)S(1)}, bf16[512,512]{1,0:T(8,128)(2,1)}, u32[]{:S(2)}) copy-start(bf16[512,512]{1,0:T(8,128)(2,1)} %param.14) | copy-start | bytes 1572868
  41.0 11.4 %copy-start.38 = (s32[512]{0:T(512)S(1)}, s32[512]{0:T(512)}, u32[]{:S(2)}) copy-start(s32[512]{0:T(512)} %param.15) | copy-start | bytes 6148
  41.0 11.4 %copy-start.37 = (s32[512]{0:T(512)S(1)}, s32[512]{0:T(512)}, u32[]{:S(2)}) copy-start(s32[512]{0:T(512)} %param.16) | copy-start | bytes 6148
  41.0 13.9 %copy-start.2 = (bf16[1024,512]{1,0:T(8,128)(2,1)S(1)}, bf16[1024,512]{1,0:T(8,128)(2,1)}, u32[]{:S(2)}) copy-start(bf16[1024,512]{1,0:T(8,128)(2,1)} %all-gather.3.cloned.1.call-done) | copy-start | bytes 3145732
  41.0 26.3 %all-to-all-start = ((bf16[32,16,512]{2,1,0:T(8,128)(2,1)}), bf16[32,16,512]{2,1,0:T(8,128)(2,1)S(1)}, u32[]{:S(2)}, u32[]{:S(2)}) async-start(bf16[32,16,512]{2,1,0:T(8,128)(2,1)} %bitcast.5), calls=%async_computation | async-start | bytes 1048576 | tf_op jit(solution)/shard_map/all_to_all | solution.py:116
  51.3 63.7 %reduce-scatter.4.cloned.1.call-start = ((), (), s32[]{:S(2)}) async-start(), calls=%async_computation.5 | async-start | bytes 2359296 | tf_op jit(solution)/shard_map/reduce_scatter | solution.py:126
  52.4 5.1 copy-start.35
  76.7 6.9 %copy-start.4 = (bf16[512,512]{0,1:T(8,128)(2,1)}, bf16[512,512]{0,1:T(8,128)(2,1)S(1)}, u32[]{:S(2)}) copy-start(bf16[512,512]{0,1:T(8,128)(2,1)S(1)} %add_convert_fusion) | copy-start | bytes 1572868
  77.9 6.0 %copy-start.16 = (bf16[128,512]{1,0:T(8,128)(2,1)S(1)}, bf16[128,512]{1,0:T(8,128)(2,1)}, u32[]{:S(2)}) copy-start(bf16[128,512]{1,0:T(8,128)(2,1)} %param.13) | copy-start | bytes 393220
  83.6 34.5 %copy-start.26 = (bf16[128,512]{1,0:T(8,128)(2,1)S(1)}, bf16[128,512]{1,0:T(8,128)(2,1)}, u32[]{:S(2)}) copy-start(bf16[128,512]{1,0:T(8,128)(2,1)} %param.24) | copy-start | bytes 393220
  83.6 34.5 %copy-start.39 = (f32[1,512]{1,0:T(1,128)S(1)}, f32[1,512]{1,0:T(1,128)}, u32[]{:S(2)}) copy-start(f32[1,512]{1,0:T(1,128)} %param.23) | copy-start | bytes 6148
  83.7 63.2 %all-gather.5.cloned.1.call-start = ((), (), s32[]{:S(2)}) async-start(), calls=%async_computation.6 | async-start | bytes 1179648 | tf_op jit(solution)/shard_map/all_gather | solution.py:175
  115.0 4.0 copy-start.44
  116.4 2.9 copy-start.22
  117.9 2.4 copy-start.40
  117.9 2.4 copy-start.30
  118.1 2.2 copy-start.41
  121.7 30.9 %copy-start.6 = (bf16[512,512]{0,1:T(8,128)(2,1)}, bf16[512,512]{0,1:T(8,128)(2,1)S(1)}, u32[]{:S(2)}) copy-start(bf16[512,512]{0,1:T(8,128)(2,1)S(1)} %copy.44) | copy-start | bytes 1572868
  130.6 16.3 %copy-start.36 = (s32[1024]{0:T(1024)S(1)}, s32[1024]{0:T(1024)}, u32[]{:S(2)}) copy-start(s32[1024]{0:T(1024)} %copy-done.35) | copy-start | bytes 12292
  134.1 18.1 %copy-start.29 = (f32[512]{0:T(512)S(1)}, f32[512]{0:T(512)}, u32[]{:S(2)}) copy-start(f32[512]{0:T(512)} %copy-done.28) | copy-start | bytes 6148
  134.1 18.1 %copy-start.32 = (f32[512]{0:T(512)S(1)}, f32[512]{0:T(512)}, u32[]{:S(2)}) copy-start(f32[512]{0:T(512)} %copy-done.31) | copy-start | bytes 6148
  134.1 18.1 %copy-start.34 = (f32[1,512]{1,0:T(1,128)S(1)}, f32[1,512]{1,0:T(1,128)}, u32[]{:S(2)}) copy-start(f32[1,512]{1,0:T(1,128)} %param.20) | copy-start | bytes 6148
  168.3 11.4 %copy-start.21 = (f32[512,512]{1,0:T(8,128)S(1)}, f32[512,512]{1,0:T(8,128)}, u32[]{:S(2)}) copy-start(f32[512,512]{1,0:T(8,128)} %copy-done.19) | copy-start | bytes 3145732
  168.3 11.4 %copy-start.25 = (bf16[512,512]{0,1:T(8,128)(2,1)S(1)}, bf16[512,512]{0,1:T(8,128)(2,1)}, u32[]{:S(2)}) copy-start(bf16[512,512]{0,1:T(8,128)(2,1)} %copy-done.24) | copy-start | bytes 1572868
  169.1 26.2 %all-to-all-start.1 = ((bf16[32,16,512]{2,1,0:T(8,128)(2,1)}), bf16[32,16,512]{2,1,0:T(8,128)(2,1)}, u32[]{:S(2)}, u32[]{:S(2)}) async-start(bf16[32,16,512]{2,1,0:T(8,128)(2,1)} %bitcast.12), calls=%async_computation.2 | async-start | bytes 1048576 | tf_op jit(solution)/shard_map/all_to_all | solution.py:196
  179.4 52.4 %reduce-scatter.6.cloned.1.call-start = ((), (), s32[]{:S(2)}) async-start(), calls=%async_computation.7 | async-start | bytes 1179648 | tf_op jit(solution)/shard_map/reduce_scatter | solution.py:202
  188.5 6.9 %slice-start = ((f32[1536,512]{1,0:T(8,128)}), f32[1024,512]{1,0:T(8,128)S(1)}, s32[]{:S(2)}) async-start(f32[1536,512]{1,0:T(8,128)} %scatter_custom_fusion.1), calls=%async_computation.9 | async-start | bytes 4194304 | tf_op jit(solution)/shard_map/slice | solution.py:194
  201.5 313.7 %all-reduce.3.cloned.1.call-start = ((), (), s32[]{:S(2)}) async-start(), calls=%async_computation.8 | async-start | bytes 14680064
  210.3 306.3 %copy-start.1 = (bf16[1,512,512]{2,1,0:T(8,128)(2,1)S(1)}, bf16[1,512,512]{2,1,0:T(8,128)(2,1)}, u32[]{:S(2)}) copy-start(bf16[1,512,512]{2,1,0:T(8,128)(2,1)} %param.19) | copy-start | bytes 1572868
  211.3 20.5 %copy-start.27 = (bf16[128,512]{1,0:T(8,128)(2,1)S(1)}, bf16[128,512]{1,0:T(8,128)(2,1)}, u32[]{:S(2)}) copy-start(bf16[128,512]{1,0:T(8,128)(2,1)} %param.24) | copy-start | bytes 393220
  (21 other events, 29.2 us)
Sparse Core Ops, SparseCore 0:
  9.9 27.0 all-gather.2
  83.7 31.1 reduce-scatter.3
  120.4 26.4 all-gather.4
  201.6 30.1 reduce-scatter.5
  237.3 277.8 all-reduce.2
where the time goes:
time: 525 us; the launch traced here: 523 us
  waiting for transfers between devices  383 us (73%)
  local copies, waits for them, and re-layouts  46 us (9%)
  other arithmetic  37 us (7%)
  matrix products  21.8 us (4%)
  starting transfers between devices  21.1 us (4%)
  between operations  14.4 us (3%)
    unnamed x6, waiting for transfers between devices  282 us
    reduce_scatter x1, waiting for transfers between devices, body(): lax.psum_scatter(partial_sum, 'esplit', scatter_dimension=0, tiled=True)  29.8 us
    all_gather x1, waiting for transfers between devices, body(): gathered = lax.all_gather(node_state, 'esplit', axis=0, tiled=True)  28.1 us
    unnamed x100, local copies, waits for them, and re-layouts  22.7 us
    reduce_scatter x1, waiting for transfers between devices, body(): lax.psum_scatter(local_grad.astype(jnp.bfloat16), 'esplit', scatter_dimen...  17.9 us
    all_gather x1, waiting for transfers between devices, body(): agg_full = lax.all_gather(grad_agg, 'esplit', axis=0, tiled=True)  12.8 us
  transfers between devices with their start and end apart: 7, of which 7 were waited for; matrix products, arithmetic and copies ran while one was open for 9% of the time, Pallas kernels for 0%

commit v1 on v0

v1 whole, which is shorter than its diff:
```python
import functools

import jax
import jax.numpy as jnp
from jax import lax
from jax.experimental import pallas as pl
from jax.experimental.pallas import tpu as pltpu
from jax.sharding import PartitionSpec as P

EPSILON = 1e-05
BF = jnp.bfloat16
F32 = jnp.float32
MESH = pl.DeviceIdType.MESH

NZ = 8
NY = 4
NX = 4
DOM = NY * NZ
S = NX * 2
D = 512
N = 128
PN = N * S
E = 512
GH = 16
SLAB = DOM // S * GH
NJ = DOM // S
HALF = D // 2
NMAT = 7
OUT_ROWS = 14


def dot(a, b):
    return lax.dot_general(a, b, (((1,), (0,)), ((), ())), preferred_element_type=F32)


def dot_nt(a, b):
    return lax.dot_general(a, b, (((1,), (1,)), ((), ())), preferred_element_type=F32)


def dot_tn(a, b):
    return lax.dot_general(a, b, (((0,), (0,)), ((), ())), preferred_element_type=F32)


def normalize(values, gain):
    average = jnp.mean(values, axis=-1, keepdims=True)
    centered = values - average
    inv_scale = lax.rsqrt(jnp.mean(centered * centered, axis=-1, keepdims=True) + EPSILON)
    return gain * centered * inv_scale


def normalize_back(values, gain, upstream):
    average = jnp.mean(values, axis=-1, keepdims=True)
    centered = values - average
    inv_scale = lax.rsqrt(jnp.mean(centered * centered, axis=-1, keepdims=True) + EPSILON)
    scaled = centered * inv_scale
    grad_scaled = upstream * gain
    first = jnp.mean(grad_scaled, axis=-1, keepdims=True)
    second = jnp.mean(grad_scaled * scaled, axis=-1, keepdims=True)
    return inv_scale * (grad_scaled - first - scaled * second)


def swish(values):
    return values * jax.nn.sigmoid(values)


def swish_slope(values):
    sigma = jax.nn.sigmoid(values)
    return sigma * (1.0 + values * (1.0 - sigma))


def rows_loop(total, step, fn):
    def one(i, carry):
        fn(pl.multiple_of(i * step, step))
        return carry

    lax.fori_loop(0, total // step, one, 0)


class Sems:
    def __init__(self, ref):
        self.ref = ref
        self.used = 0

    def take(self, count):
        base = self.used
        self.used += count
        return lambda i: self.ref.at[base + i]


N_SEM = 200


def kernel(
    nodes_in, snd_row, rcv_row, lst_row, egain, ngain, ncot,
    edges_hbm, ein_hbm, eout_hbm, nin_hbm, nout_hbm, ecot_hbm,
    nodes_out, edges_out, ngrad, egrad, wout,
    edges, ein, eout, nin, nout, ecot,
    ps, pr, pst, prt, tbl, sent_acc, sent, recv, pre, msg, hid,
    gsend, aggs_send, aggs_recv, aggx_send, aggx_recv, agg_own,
    agg, npre, nhid, gdirect, dnpre, dnmsg, dagg_own, dagg,
    gedge, dmsg, dpre, dsent, drecv,
    gg_ssend, gg_srecv, gg_xsend, gg_xrecv, gg_own, a2_send, retg,
    own_ssend, own_srecv, own_xsend, own_xrecv, own_own,
    fn_ssend, fn_srecv, fn_own, fn_ysend, fn_yrecv, fn_zsend, fn_zrecv,
    fe_ssend, fe_srecv, fe_own, fe_ysend, fe_yrecv, fe_zsend, fe_zrecv,
    fin, g1_recv, g2_src, g2_recv,
    sem_ref,
):
    d = lax.axis_index("dom")
    s = lax.axis_index("esplit")
    y = d // NZ
    z = d % NZ
    x = s // 2
    c = s % 2
    lin = d * S + s
    sib = s + 1 - 2 * c
    t_mine = (s - d + DOM) % S
    sems = Sems(sem_ref)
    pending = []

    def remote(src, dst, send_sem, recv_sem, dom, split):
        return pltpu.make_async_remote_copy(
            src_ref=src, dst_ref=dst, send_sem=send_sem, recv_sem=recv_sem,
            device_id=(dom, split), device_id_type=MESH,
        )

    bar = pltpu.get_barrier_semaphore()

    def greet(dom, split):
        pl.semaphore_signal(bar, inc=1, device_id=(dom, split), device_id_type=MESH)

    for k in range(1, S):
        greet(d, (s + k) % S)
    for k in range(1, NY):
        greet((y + k) % NY * NZ + z, s)
    for k in range(1, NZ):
        greet(y * NZ + (z + k) % NZ, s)
    for j in range(NJ):
        pl.when(t_mine + S * j != d)(functools.partial(greet, t_mine + S * j, s))
    first_row = OUT_ROWS * lin
    b_first = first_row // 16
    b_last = (first_row + OUT_ROWS - 1) // 16
    b_mine = DOM * s + d
    l_first = (16 * b_mine) // OUT_ROWS
    l_last = (16 * b_mine + 15) // OUT_ROWS

    def block_lin(b):
        return (b % DOM) * S + b // DOM

    pl.when(block_lin(b_first) != lin)(
        functools.partial(greet, b_first % DOM, b_first // DOM))
    pl.when((b_last != b_first) & (block_lin(b_last) != lin))(
        functools.partial(greet, b_last % DOM, b_last // DOM))

    lsem = sems.take(6)
    loads = [
        pltpu.make_async_copy(a, b, lsem(i))
        for i, (a, b) in enumerate(
            ((edges_hbm, edges), (ein_hbm, ein), (eout_hbm, eout), (nin_hbm, nin),
             (nout_hbm, nout), (ecot_hbm, ecot)))
    ]
    for load in loads:
        load.start()

    tbl[pl.ds(pl.multiple_of(s * N, N), N), :] = nodes_in[...]

    def g2_valid(i):
        return (s < NMAT) & (l_first + i <= l_last) & (l_first + i != lin)

    arrivals = (S - 1) + (NY - 1) + (NZ - 1)
    for j in range(NJ):
        arrivals = arrivals + jnp.where(t_mine + S * j != d, 1, 0)
    for i in range(3):
        arrivals = arrivals + jnp.where(g2_valid(i), 1, 0)
    pl.semaphore_wait(bar, arrivals)

    class Gather:
        def __init__(self, buf, offset, rows):
            self.buf, self.offset, self.rows = buf, offset, rows
            self.ss, self.rs = sems.take(7), sems.take(7)

        def block(self, split):
            return self.buf.at[pl.ds(pl.multiple_of(self.offset(split), self.rows), self.rows), :]

        def copy(self, origin, k, split, src=None):
            blk = self.block(origin)
            return remote(blk if src is None else src, blk, self.ss(k), self.rs(k), d, split)

        def start(self, src=None):
            for dx in (2, 1, 3):
                cp = self.copy(s, dx - 1, (x + dx) % NX * 2 + c, src)
                cp.start()
                pending.append(cp)
            cp = self.copy(s, 3, sib, src)
            cp.start()
            pending.append(cp)

        def forward(self, dx):
            origin = (x - dx + NX) % NX * 2 + c
            self.copy(origin, dx - 1, sib).wait_recv()
            cp = self.copy(origin, 3 + dx, sib)
            cp.start()
            pending.append(cp)

        def from_sib(self, dx):
            if dx == 0:
                self.copy(sib, 3, sib).wait_recv()
            else:
                self.copy((x - dx + NX) % NX * 2 + 1 - c, 3 + dx, sib).wait_recv()

        def finish(self):
            for dx in (1, 3, 2):
                self.forward(dx)
            for dx in (0, 1, 3, 2):
                self.from_sib(dx)

    class Scatter:
        def __init__(self, compute, own, ssend, srecv, xsend, xrecv):
            self.compute, self.own = compute, own
            self.ssend, self.srecv, self.xsend, self.xrecv = ssend, srecv, xsend, xrecv
            self.s1, self.r1 = sems.take(4), sems.take(4)
            self.s2, self.r2 = sems.take(3), sems.take(3)

        def to_sib(self, dx):
            return remote(self.ssend.at[dx], self.srecv.at[dx], self.s1(dx), self.r1(dx), d, sib)

        def to_chip(self, dx):
            return remote(
                self.xsend.at[dx - 1], self.xrecv.at[dx - 1], self.s2(dx - 1), self.r2(dx - 1),
                d, (x + dx) % NX * 2 + c)

        def start(self):
            for dx in (2, 1, 3, 0):
                self.ssend[dx] = self.compute((x + dx) % NX * 2 + 1 - c).astype(BF)
                cp = self.to_sib(dx)
                cp.start()
                pending.append(cp)

        def middle(self):
            for dx in (2, 1, 3):
                mine = self.compute((x + dx) % NX * 2 + c)
                self.to_sib(dx).wait_recv()
                self.xsend[dx - 1] = (mine + self.srecv[dx].astype(F32)).astype(BF)
                cp = self.to_chip(dx)
                cp.start()
                pending.append(cp)
            mine = self.compute(s)
            self.to_sib(0).wait_recv()
            self.own[...] = mine + self.srecv[0].astype(F32)

        def finish(self):
            total = self.own[...]
            for dx in (1, 3, 2):
                self.to_chip(dx).wait_recv()
                total = total + self.xrecv[dx - 1].astype(F32)
            return total

    class Swap:
        def __init__(self, src, dst):
            self.src, self.dst = src, dst
            self.ss, self.rs = sems.take(NJ), sems.take(NJ)

        def start(self):
            for j in range(NJ):
                peer = t_mine + S * j
                land = pl.multiple_of((d % S) * SLAB + (d // S) * GH, GH)
                cp = remote(
                    self.src.at[pl.ds(j * GH, GH), :], self.dst.at[pl.ds(land, GH), :],
                    self.ss(j), self.rs(d // S), peer, s)
                pl.when(peer != d)(cp.start)

                @pl.when(peer == d)
                def _():
                    self.dst[pl.ds(land, GH), :] = self.src[pl.ds(j * GH, GH), :]

        def finish(self):
            for j in range(NJ):
                peer = t_mine + S * j
                land = pl.multiple_of(t_mine * SLAB + j * GH, GH)
                cp = remote(
                    self.src.at[pl.ds(j * GH, GH), :], self.dst.at[pl.ds(land, GH), :],
                    self.ss(j), self.rs(j), peer, s)

                @pl.when(peer != d)
                def _():
                    cp.wait_recv()
                    cp.wait_send()

    gather_nodes = Gather(tbl, lambda q: q * N, N)
    gather_nodes.start(nodes_in)

    def permuted(values):
        ghost = values - PN
        part = ghost // GH
        place = PN + (part % S) * SLAB + (part // S) * GH + ghost % GH
        return jnp.where(values >= PN, place, values)

    def column(row):
        size = row.shape[1]
        hit = lax.broadcasted_iota(jnp.int32, (size, size), 0) == lax.broadcasted_iota(
            jnp.int32, (size, size), 1)
        return jnp.sum(jnp.where(hit, row.astype(F32), 0.0), axis=1, keepdims=True).astype(jnp.int32)

    def hot(mask):
        return jnp.where(mask, 1.0, 0.0).astype(BF)

    send_r = permuted(snd_row[...])
    recv_r = rcv_row[...]
    send_c = column(send_r)
    recv_c = column(recv_r)

    def build_t(r0):
        ids = lax.broadcasted_iota(jnp.int32, (256, E), 0) + r0
        pst[pl.ds(r0, 256), :] = hot(ids == send_r)

    rows_loop(PN + S * SLAB, 256, build_t)

    def build_rt(r0):
        ids = lax.broadcasted_iota(jnp.int32, (256, E), 0) + r0
        prt[pl.ds(r0, 256), :] = hot(ids == recv_r)

    rows_loop(PN, 256, build_rt)
    for c0 in range(0, PN + S * SLAB, 256):
        ids = lax.broadcasted_iota(jnp.int32, (E, 256), 1) + c0
        ps[:, c0:c0 + 256] = hot(ids == send_c)
        if c0 < PN:
            pr[:, c0:c0 + 256] = hot(ids == recv_c)
    lists_c = column(lst_row[...])

    loads[0].wait()
    loads[1].wait()

    def edge_part(r0):
        pre[pl.ds(r0, 256), :] = dot(edges[pl.ds(r0, 256), :], ein[0])

    rows_loop(E, 256, edge_part)

    gather_nodes.finish()

    hit = jnp.zeros((SLAB, 1), jnp.int32)
    for t in range(S):
        hit = jnp.where(t_mine == t, lists_c[t * SLAB:(t + 1) * SLAB, :], hit)
    pick = hot(lax.broadcasted_iota(jnp.int32, (SLAB, PN), 1) == hit)
    gsend[...] = dot(pick, tbl[:PN, :]).astype(BF)
    ghosts = tbl.at[pl.ds(PN, S * SLAB), :]
    swap_ghost = Swap(gsend, ghosts)
    swap_ghost.start()

    def gather_rows(r0):
        rows = pl.ds(r0, 256)
        got = dot(pr[rows, :], tbl[:PN, :]).astype(BF)
        recv[rows, :] = got
        pre[rows, :] = pre[rows, :] + dot(got, ein[2])
        sent_acc[rows, :] = dot(ps[rows, :PN], tbl[:PN, :])

    rows_loop(E, 256, gather_rows)
    swap_ghost.finish()
    gather_ghost = Gather(ghosts, lambda q: ((q - d + DOM) % S) * SLAB, SLAB)
    gather_ghost.start()
    gather_ghost.finish()

    loads[2].wait()
    edge_gain = egain[...]

    def edge_forward(r0):
        rows = pl.ds(r0, 256)
        got = (sent_acc[rows, :] + dot(ps[rows, PN:], tbl[PN:, :])).astype(BF)
        sent[rows, :] = got
        act = pre[rows, :] + dot(got, ein[1])
        pre[rows, :] = act
        hidden = swish(act).astype(BF)
        hid[rows, :] = hidden
        message = dot(hidden, eout[...])
        msg[rows, :] = message
        edges_out[rows, :] = (edges[rows, :].astype(F32) + normalize(message, edge_gain)).astype(BF)

    rows_loop(E, 256, edge_forward)

    def agg_block(q):
        return dot(prt[pl.ds(pl.multiple_of(q * N, N), N), :], edges_out[...])

    reduce_agg = Scatter(agg_block, agg_own, aggs_send, aggs_recv, aggx_send, aggx_recv)
    reduce_agg.start()
    reduce_agg.middle()
    loads[3].wait()
    loads[4].wait()
    loads[5].wait()
    npre[...] = dot(nodes_in[...], nin[0])
    agg[...] = reduce_agg.finish().astype(BF)

    node_gain = ngain[...]
    act = npre[...] + dot(agg[...], nin[1])
    hidden = swish(act).astype(BF)
    nhid[...] = hidden
    message = dot(hidden, nout[...])
    nodes_out[...] = (nodes_in[...].astype(F32) + normalize(message, node_gain)).astype(BF)
    upstream = ncot[...].astype(F32)
    grad_message = normalize_back(message, node_gain, upstream).astype(BF)
    dnmsg[...] = grad_message
    grad_pre = (dot_nt(grad_message, nout[...]) * swish_slope(act)).astype(BF)
    dnpre[...] = grad_pre
    dagg_own[...] = dot_nt(grad_pre, nin[1]).astype(BF)
    dagg[pl.ds(pl.multiple_of(s * N, N), N), :] = dagg_own[...]

    gather_dagg = Gather(dagg, lambda q: q * N, N)
    gather_dagg.start(dagg_own)
    gdirect[...] = upstream + dot_nt(grad_pre, nin[0])

    mine_cols = pl.ds(pl.multiple_of(c * HALF, HALF), HALF)
    sib_cols = pl.ds(pl.multiple_of((1 - c) * HALF, HALF), HALF)

    class Weights:
        def __init__(self, base, pairs, ssend, srecv, own, ysend, yrecv, zsend, zrecv):
            self.base, self.pairs = base, pairs
            self.ssend, self.srecv, self.own = ssend, srecv, own
            self.ysend, self.yrecv, self.zsend, self.zrecv = ysend, yrecv, zsend, zrecv
            self.s0, self.r0 = sems.take(len(pairs)), sems.take(len(pairs))
            self.sy, self.ry = sems.take(NY - 1), sems.take(NY - 1)
            self.sz, self.rz = sems.take(NZ - 1), sems.take(NZ - 1)

        def sib_copy(self, i):
            return remote(self.ssend.at[i], self.srecv.at[i], self.s0(i), self.r0(i), d, sib)

        def y_copy(self, k):
            return remote(
                self.ysend.at[k], self.yrecv.at[k - 1], self.sy(k - 1), self.ry(k - 1),
                (y + k) % NY * NZ + z, s)

        def z_copy(self, k):
            return remote(
                self.zsend.at[k], self.zrecv.at[k - 1], self.sz(k - 1), self.rz(k - 1),
                y * NZ + (z + k) % NZ, s)

        def products(self, i):
            left, right = self.pairs[i]
            self.ssend[i] = dot_tn(left[...], right[:, sib_cols]).astype(BF)
            cp = self.sib_copy(i)
            cp.start()
            pending.append(cp)
            self.own[i] = dot_tn(left[...], right[:, mine_cols])

        def to_y(self):
            for i in range(len(self.pairs)):
                self.sib_copy(i).wait_recv()
            for k in (2, 1, 3, 0):
                rows = pl.ds(pl.multiple_of((y + k) % NY * 128, 128), 128)
                for i in range(len(self.pairs)):
                    both = self.own[i, rows, :] + self.srecv[i, rows, :].astype(F32)
                    self.ysend[k, i] = both.astype(BF)
                if k:
                    cp = self.y_copy(k)
                    cp.start()
                    pending.append(cp)

        def to_z(self):
            for k in range(1, NY):
                self.y_copy(k).wait_recv()
            for k in (4, 3, 5, 2, 6, 1, 7, 0):
                rows = pl.ds(pl.multiple_of((z + k) % NZ * 16, 16), 16)
                for i in range(len(self.pairs)):
                    total = self.ysend[0, i, rows, :].astype(F32)
                    for q in range(NY - 1):
                        total = total + self.yrecv[q, i, rows, :].astype(F32)
                    self.zsend[k, i] = total.astype(BF)
                if k:
                    cp = self.z_copy(k)
                    cp.start()
                    pending.append(cp)

        def finish(self):
            for k in range(1, NZ):
                self.z_copy(k).wait_recv()
            for i in range(len(self.pairs)):
                total = self.zsend[0, i].astype(F32)
                for k in range(NZ - 1):
                    total = total + self.zrecv[k, i].astype(F32)
                fin[self.base + i] = total

    node_weights = Weights(
        4, ((nodes_in, dnpre), (agg, dnpre), (nhid, dnmsg)),
        fn_ssend, fn_srecv, fn_own, fn_ysend, fn_yrecv, fn_zsend, fn_zrecv)
    edge_weights = Weights(
        0, ((edges, dpre), (sent, dpre), (recv, dpre), (hid, dmsg)),
        fe_ssend, fe_srecv, fe_own, fe_ysend, fe_yrecv, fe_zsend, fe_zrecv)

    for i in range(3):
        node_weights.products(i)
    for dx in (1, 3, 2):
        gather_dagg.forward(dx)
    node_weights.to_y()
    for dx in (0, 1, 3, 2):
        gather_dagg.from_sib(dx)

    def edge_backward(r0):
        rows = pl.ds(r0, 256)
        up = ecot[rows, :].astype(F32) + dot(pr[rows, :], dagg[...])
        gedge[rows, :] = up
        grad_msg = normalize_back(msg[rows, :], edge_gain, up).astype(BF)
        dmsg[rows, :] = grad_msg
        grad = (dot_nt(grad_msg, eout[...]) * swish_slope(pre[rows, :])).astype(BF)
        dpre[rows, :] = grad
        dsent[rows, :] = dot_nt(grad, ein[1]).astype(BF)

    rows_loop(E, 256, edge_backward)

    def ghost_block(q):
        place = PN + ((q - d + DOM) % S) * SLAB
        return dot(pst[pl.ds(pl.multiple_of(place, SLAB), SLAB), :], dsent[...])

    reduce_ghost = Scatter(
        ghost_block, gg_own, gg_ssend, gg_srecv, gg_xsend, gg_xrecv)
    reduce_ghost.start()
    edge_weights.products(3)
    reduce_ghost.middle()
    for i in range(3):
        edge_weights.products(i)
    edge_weights.to_y()

    def recv_grad(r0):
        rows = pl.ds(r0, 256)
        drecv[rows, :] = dot_nt(dpre[rows, :], ein[2]).astype(BF)

    rows_loop(E, 256, recv_grad)
    a2_send[...] = reduce_ghost.finish().astype(BF)
    swap_back = Swap(a2_send, retg)
    swap_back.start()

    def own_block(q):
        rows = pl.ds(pl.multiple_of(q * N, N), N)
        return dot(pst[rows, :], dsent[...]) + dot(prt[rows, :], drecv[...])

    reduce_own = Scatter(
        own_block, own_own, own_ssend, own_srecv, own_xsend, own_xrecv)
    reduce_own.start()
    swap_back.finish()
    gather_back = Gather(retg, lambda q: ((q - d + DOM) % S) * SLAB, SLAB)
    gather_back.start()
    reduce_own.middle()
    node_weights.to_z()
    for dx in (1, 3, 2):
        gather_back.forward(dx)
    edge_weights.to_z()

    def edge_grad(r0):
        rows = pl.ds(r0, 256)
        egrad[rows, :] = (gedge[rows, :] + dot_nt(dpre[rows, :], ein[0])).astype(BF)

    rows_loop(E, 256, edge_grad)
    place = hot(lax.broadcasted_iota(jnp.int32, (N, S * SLAB), 0) + s * N == lst_row[...])
    for dx in (0, 1, 3, 2):
        gather_back.from_sib(dx)
    ngrad[...] = (gdirect[...] + dot(place, retg[...]) + reduce_own.finish()).astype(BF)

    node_weights.finish()
    edge_weights.finish()
    s_g1, r_g1 = sems.take(S - 1), sems.take(S - 1)

    def g1_copy(k):
        peer = (s + k) % S
        which = jnp.minimum(peer, NMAT - 1)
        return remote(fin.at[which], g1_recv.at[k - 1], s_g1(k - 1), r_g1(k - 1), d, peer)

    for k in range(1, S):
        cp = g1_copy(k)
        pl.when((s + k) % S < NMAT)(cp.start)
    s_g2, r_g2 = sems.take(3), sems.take(2)

    def g2_copy(i, slot):
        to = l_first + i
        to = jnp.minimum(to, DOM * S - 1)
        return remote(g2_src, g2_recv.at[slot], s_g2(i), r_g2(slot), to // S, to % S)

    @pl.when(s < NMAT)
    def _():
        for k in range(1, S):
            g1_copy(k).wait_recv()
        for half in range(2):
            total = fin[jnp.minimum(s, NMAT - 1)]
            total = jnp.where(c == half, total, 0.0)
            for k in range(1, S):
                origin = (s - k + S) % S
                total = total + jnp.where(origin % 2 == half, g1_recv[k - 1], 0.0)
            g2_src[:, half * HALF:(half + 1) * HALF] = total
        for i in range(3):
            to = l_first + i
            slot = b_mine - (OUT_ROWS * to) // 16
            for choice in range(2):
                pl.when(g2_valid(i) & (slot == choice))(g2_copy(i, choice).start)

                @pl.when((to <= l_last) & (to == lin) & (slot == choice))
                def _():
                    g2_recv[choice] = g2_src[...]

    pl.when(block_lin(b_first) != lin)(g2_copy(0, 0).wait_recv)
    pl.when((b_last != b_first) & (block_lin(b_last) != lin))(g2_copy(0, 1).wait_recv)
    shift = first_row % 16
    for choice in range(0, 16, 2):
        @pl.when(shift == choice)
        def _():
            split = min(16 - choice, OUT_ROWS)
            wout[:split, :] = g2_recv[0, choice:choice + split, :]
            if split < OUT_ROWS:
                wout[split:, :] = g2_recv[1, :OUT_ROWS - split, :]

    for cp in pending:
        cp.wait_send()
    for k in range(1, S):
        pl.when((s + k) % S < NMAT)(g1_copy(k).wait_send)
    for i in range(3):
        pl.when(g2_valid(i))(g2_copy(i, 0).wait_send)


def scratch():
    def bf(*shape):
        return pltpu.VMEM(shape, BF)

    def f32(*shape):
        return pltpu.VMEM(shape, F32)

    T = PN + S * SLAB

    def scatter(rows):
        return [bf(NX, rows, D), bf(NX, rows, D), bf(NX - 1, rows, D), bf(NX - 1, rows, D)]

    def weights(count):
        return [
            bf(count, D, HALF), bf(count, D, HALF), f32(count, D, HALF),
            bf(NY, count, 128, HALF), bf(NY - 1, count, 128, HALF),
            bf(NZ, count, 16, HALF), bf(NZ - 1, count, 16, HALF),
        ]

    return [
        bf(E, D), bf(3, D, D), bf(D, D), bf(2, D, D), bf(D, D), bf(E, D),
        bf(E, T), bf(E, PN), bf(T, E), bf(PN, E), bf(T, D), f32(E, D), bf(E, D), bf(E, D),
        f32(E, D), f32(E, D), bf(E, D),
        bf(SLAB, D), *scatter(N), f32(N, D),
        bf(N, D), f32(N, D), bf(N, D), f32(N, D), bf(N, D), bf(N, D), bf(N, D), bf(PN, D),
        f32(E, D), bf(E, D), bf(E, D), bf(E, D), bf(E, D),
        *scatter(SLAB), f32(SLAB, D), bf(SLAB, D), bf(S * SLAB, D),
        *scatter(N), f32(N, D),
        *weights(3), *weights(4),
        f32(NMAT, 16, HALF), f32(S - 1, 16, HALF), f32(16, D), f32(2, 16, D),
        pltpu.SemaphoreType.DMA((N_SEM,)),
    ]


def hand_over(a0, a1, a2, a3, w_in, b0, b1, b2, b3, w_out, sem):
    copies = [
        pltpu.make_async_copy(src, dst, sem.at[i])
        for i, (src, dst) in enumerate(((a0, b0), (a1, b1), (a2, b2), (a3, b3)))
    ]
    for cp in copies:
        cp.start()
    for i in range(OUT_ROWS):
        w_out[:, i * D:(i + 1) * D] = w_in[i:i + 1, :]
    for cp in copies:
        cp.wait()


def body(
    node_state, edge_state, senders, receivers, send_rows, edge_in, edge_out, edge_gain,
    node_in, node_out, node_gain, node_cot, edge_cot,
):
    lists = send_rows.reshape(NJ, S, GH).transpose(1, 0, 2).reshape(1, S * SLAB)
    vmem = pl.BlockSpec(memory_space=pltpu.VMEM)
    hbm = pl.BlockSpec(memory_space=pl.ANY)
    states = (
        jax.ShapeDtypeStruct((N, D), BF),
        jax.ShapeDtypeStruct((E, D), BF),
        jax.ShapeDtypeStruct((N, D), BF),
        jax.ShapeDtypeStruct((E, D), BF),
    )
    results = pl.pallas_call(
        kernel,
        out_shape=states + (jax.ShapeDtypeStruct((OUT_ROWS, D), F32),),
        in_specs=[vmem] * 7 + [hbm] * 6,
        out_specs=[vmem] * 5,
        scratch_shapes=scratch(),
        compiler_params=pltpu.CompilerParams(
            collective_id=0, has_side_effects=True, vmem_limit_bytes=60 * 1024 * 1024),
    )(
        node_state, senders.reshape(1, E), receivers.reshape(1, E), lists,
        edge_gain, node_gain, node_cot,
        edge_state, edge_in[0], edge_out[0], node_in[0], node_out[0], edge_cot,
    )
    return pl.pallas_call(
        hand_over,
        out_shape=states + (jax.ShapeDtypeStruct((1, OUT_ROWS * D), F32),),
        in_specs=[hbm] * 4 + [vmem],
        out_specs=[hbm] * 4 + [vmem],
        scratch_shapes=[pltpu.SemaphoreType.DMA((4,))],
    )(*results)


def solution(mesh):
    both = P(("dom", "esplit"), None)
    in_specs = (
        both, both, P(("dom", "esplit")), P(("dom", "esplit")), P("dom", None, None),
        P(), P(), P(), P(), P(), P(), both, both,
    )
    out_specs = (both, both, both, both, P(None, ("dom", "esplit")))
    return jax.shard_map(body, mesh=mesh, in_specs=in_specs, out_specs=out_specs, check_vma=False)
```

time: 525 us -> 142 us (0.27)
  waiting for transfers between devices: 383 us -> 0 us
  Pallas kernels: 0 us -> 139 us
  local copies, waits for them, and re-layouts: 46 us -> 1.45 us
  other arithmetic: 37 us -> 0 us
  matrix products: 21.8 us -> 0 us
  starting transfers between devices: 21.1 us -> 0 us
  between operations: 14.4 us -> 0.64 us
    unnamed x6 -> x0, waiting for transfers between devices: 282 us -> none
    pallas_call x0 -> x2, Pallas kernels: none -> 139 us  [the longest x1 96.7 us: body(): pl.pallas_call(kernel, out_shape=states + (jax.ShapeDtypeStruct((OUT_ROWS...]
    reduce_scatter x2 -> x0, waiting for transfers between devices: 47.8 us -> none  [the longest x1 29.8 us: body(): lax.psum_scatter(partial_sum, 'esplit', scatter_dimension=0, tiled=True)]
    all_gather x2 -> x0, waiting for transfers between devices: 40.9 us -> none  [the longest x1 28.1 us: body(): gathered = lax.all_gather(node_state, 'esplit', axis=0, tiled=True)]
    unnamed x100 -> x1, local copies, waits for them, and re-layouts: 22.7 us -> 0.77 us
    dot_general x21 -> x0, matrix products: 21.8 us -> none  [the longest x7 7.42 us: project_back(): lax.dot_general(grad, weight, (((1,), (1,)), ((), ())), preferred_element...]
    all_to_all x2 -> x0, starting transfers between devices: 20.5 us -> none  [the longest x1 10.3 us: body(): lax.all_to_all(gathered[lists], 'dom', split_axis=0, concat_axis=0, tiled...]
    scatter-add x3 -> x0, other arithmetic: 19.9 us -> none  [the longest x1 9.32 us: body(): jax.ops.segment_sum(jnp.concatenate([grad_sent, grad_recv]), jnp.concaten...]
  transfers between devices with their start and end apart: 7 -> 0, of which waited for: 7 -> 0; matrix products, arithmetic and copies ran while one was open for 9% -> 0% of each run, Pallas kernels for 0% -> 0%
where the time goes in v1:
time: 142 us; the launch traced here: 141 us
  Pallas kernels  139 us (98%)
  local copies, waits for them, and re-layouts  1.45 us (1%)
    pallas_call x1, Pallas kernels, body(): pl.pallas_call(kernel, out_shape=states + (jax.ShapeDtypeStruct((OUT_ROWS...  96.7 us
    pallas_call x1, Pallas kernels, body(): pl.pallas_call(hand_over, out_shape=states + (jax.ShapeDtypeStruct((1, OU...  42.2 us

profile of v1, /device:TPU:14, one launch (start us, length us, event | category | flops | bytes accessed | tf_op | source)
XLA Modules:
  0.0 141.0 jit_solution(14692111217372704642)
XLA Ops:
  0.6 0.8 copy.19
  1.4 0.7 reshape.25.lst_row
  2.1 96.7 %shard_map.164 = (bf16[128,512]{1,0:T(8,128)(2,1)}, bf16[512,512]{1,0:T(8,128)(2,1)}, bf16[128,512]{1,0:T(8,128)(2,1)}, bf16[512,512]{1,0:T(8,128)(2,1)}, f32[14,512]{1,0:T(8,128)}) custom-call(bf16[128,512]{1,0:T(8,128)(2,1)} %nodes_in.1, s32[1,512]{1,0:T(1,128)} %bitcast.14, s32[1,512]{1,0:T(1,128)} %bitcast.15, s32[1,512]{1,0:T(1,128)} %reshape.25.lst_row, ...), custom_call_target="tpu_custom_call" | custom-call | tf_op jit(solution)/shard_map/pallas_call | solution.py:673
  98.8 42.2 %shard_map.165 = (bf16[128,512]{1,0:T(8,128)(2,1)}, bf16[512,512]{1,0:T(8,128)(2,1)}, bf16[128,512]{1,0:T(8,128)(2,1)}, bf16[512,512]{1,0:T(8,128)(2,1)}, f32[1,7168]{1,0:T(1,128)}) custom-call(bf16[128,512]{1,0:T(8,128)(2,1)} %get-tuple-element.10.a0, bf16[512,512]{1,0:T(8,128)(2,1)} %get-tuple-element.11.a1, bf16[128,512]{1,0:T(8,128)(2,1)} %get-tuple-element.12.a2, ...), custom_call_target="tpu_custom_call" | custom-call | tf_op jit(solution)/shard_map/pallas_call | solution.py:686
  (1 shorter events, 0.0 us)

commit v2 on v1

v2 whole, which is shorter than its diff:
```python
import functools

import jax
import jax.numpy as jnp
from jax import lax
from jax.experimental import pallas as pl
from jax.experimental.pallas import tpu as pltpu
from jax.sharding import PartitionSpec as P

EPSILON = 1e-05
BF = jnp.bfloat16
F32 = jnp.float32
MESH = pl.DeviceIdType.MESH

NZ = 8
NY = 4
NX = 4
DOM = NY * NZ
S = NX * 2
D = 512
N = 128
PN = N * S
E = 512
GH = 16
SLAB = DOM // S * GH
NJ = DOM // S
HALF = D // 2
NMAT = 7
OUT_ROWS = 14


def dot(a, b):
    return lax.dot_general(a, b, (((1,), (0,)), ((), ())), preferred_element_type=F32)


def dot_nt(a, b):
    return lax.dot_general(a, b, (((1,), (1,)), ((), ())), preferred_element_type=F32)


def dot_tn(a, b):
    return lax.dot_general(a, b, (((0,), (0,)), ((), ())), preferred_element_type=F32)


def normalize(values, gain):
    average = jnp.mean(values, axis=-1, keepdims=True)
    centered = values - average
    inv_scale = lax.rsqrt(jnp.mean(centered * centered, axis=-1, keepdims=True) + EPSILON)
    return gain * centered * inv_scale


def normalize_back(values, gain, upstream):
    average = jnp.mean(values, axis=-1, keepdims=True)
    centered = values - average
    inv_scale = lax.rsqrt(jnp.mean(centered * centered, axis=-1, keepdims=True) + EPSILON)
    scaled = centered * inv_scale
    grad_scaled = upstream * gain
    first = jnp.mean(grad_scaled, axis=-1, keepdims=True)
    second = jnp.mean(grad_scaled * scaled, axis=-1, keepdims=True)
    return inv_scale * (grad_scaled - first - scaled * second)


def swish(values):
    return values * jax.nn.sigmoid(values)


def swish_slope(values):
    sigma = jax.nn.sigmoid(values)
    return sigma * (1.0 + values * (1.0 - sigma))


def rows_loop(total, step, fn):
    def one(i, carry):
        fn(pl.multiple_of(i * step, step))
        return carry

    lax.fori_loop(0, total // step, one, 0)


class Sems:
    def __init__(self, ref):
        self.ref = ref
        self.used = 0

    def take(self, count):
        base = self.used
        self.used += count
        return lambda i: self.ref.at[base + i]


N_SEM = 280


def kernel(
    nodes_in, snd_row, rcv_row, snd_lists, egain, ngain, ncot,
    edges_hbm, ein_hbm, eout_hbm, nin_hbm, nout_hbm, ecot_hbm,
    nodes_out, edges_out, ngrad, egrad, wout,
    edges, ein, eout, nin, nout, ecot,
    ps, pr, pst, prt, tbl, sent_acc, sent, recv, pre, msg, hid,
    gsend, agg_keep, aggs_send, aggs_recv, agg_bufs,
    agg, npre, nhid, gdirect, dnpre, dnmsg, dagg_own, dagg,
    gedge, dmsg, dpre, dsent, drecv,
    gg_keep, gg_ssend, gg_srecv, gg_bufs, a2_send, retg,
    own_keep, own_ssend, own_srecv, own_bufs,
    fn_ssend, fn_srecv, fn_own, fn_ybufs, fn_ysum, fn_xbufs, fn_zsend, fn_zrecv,
    fe_ssend, fe_srecv, fe_own, fe_ybufs, fe_ysum, fe_xbufs, fe_zsend, fe_zrecv,
    fz_total, fin, rows_in,
    sem_ref,
):
    d = lax.axis_index("dom")
    s = lax.axis_index("esplit")
    y = d // NZ
    z = d % NZ
    x = s // 2
    c = s % 2
    lin = d * S + s
    sib = s + 1 - 2 * c
    t_mine = (s - d + DOM) % S
    sems = Sems(sem_ref)
    pending = []

    def remote(src, dst, send_sem, recv_sem, dom, split):
        return pltpu.make_async_remote_copy(
            src_ref=src, dst_ref=dst, send_sem=send_sem, recv_sem=recv_sem,
            device_id=(dom, split), device_id_type=MESH,
        )

    bar = pltpu.get_barrier_semaphore()

    def greet(dom, split):
        pl.semaphore_signal(bar, inc=1, device_id=(dom, split), device_id_type=MESH)

    for k in range(1, S):
        greet(d, (s + k) % S)
    for k in range(1, NY):
        greet((y + k) % NY * NZ + z, s)
    for k in range(1, NZ):
        greet(y * NZ + (z + k) % NZ, s)
    for j in range(NJ):
        pl.when(t_mine + S * j != d)(functools.partial(greet, t_mine + S * j, s))
    first_row = OUT_ROWS * lin
    b_first = first_row // 16
    b_last = (first_row + OUT_ROWS - 1) // 16

    def holder(b, half):
        return b % DOM, (b // DOM) % NX * 2 + half

    def from_other(slot, half):
        dom, split = holder(b_first + slot, half)
        here = dom * S + split != lin
        return here if slot == 0 else here & (b_last != b_first)

    for slot in range(2):
        for half in range(2):
            dom, split = holder(b_first + slot, half)
            pl.when(from_other(slot, half))(functools.partial(greet, dom, split))

    lsem = sems.take(6)
    loads = [
        pltpu.make_async_copy(a, b, lsem(i))
        for i, (a, b) in enumerate(
            ((edges_hbm, edges), (ein_hbm, ein), (eout_hbm, eout), (nin_hbm, nin),
             (nout_hbm, nout), (ecot_hbm, ecot)))
    ]
    for load in loads:
        load.start()

    tbl[pl.ds(pl.multiple_of(s * N, N), N), :] = nodes_in[...]

    def owner(group, i):
        b = DOM * (x + NX * group) + d
        to = (16 * b) // OUT_ROWS + i
        valid = to <= (16 * b + 15) // OUT_ROWS
        if group:
            valid = valid & (x < NMAT - NX)
        return to, b - (OUT_ROWS * to) // 16, valid

    arrivals = (S - 1) + (NY - 1) + (NZ - 1)
    for j in range(NJ):
        arrivals = arrivals + jnp.where(t_mine + S * j != d, 1, 0)
    for group in range(2):
        for i in range(3):
            to, _, valid = owner(group, i)
            arrivals = arrivals + jnp.where(valid & (to != lin), 1, 0)
    pl.semaphore_wait(bar, arrivals)

    def on_x(dx):
        return (x + dx + NX) % NX * 2 + c

    class Gather:
        def __init__(self, buf, offset, rows):
            self.buf, self.offset, self.rows, self.half = buf, offset, rows, rows // 2
            self.ss, self.rs = sems.take(10), sems.take(10)

        def part(self, split, half):
            start = pl.multiple_of(self.offset(split), self.rows)
            if half is None:
                return self.buf.at[pl.ds(start, self.rows), :]
            return self.buf.at[pl.ds(start + half * self.half, self.half), :]

        def copy(self, k, origin, half, split, src=None):
            there = self.part(origin, half)
            if src is None:
                here = there
            elif half is None:
                here = src
            else:
                here = src.at[pl.ds(half * self.half, self.half), :]
            return remote(here, there, self.ss(k), self.rs(k), d, split)

        def send(self, k, origin, half, split, src=None):
            cp = self.copy(k, origin, half, split, src)
            cp.start()
            pending.append(cp)

        def arrived(self, k, origin, half):
            self.copy(k, origin, half, sib).wait_recv()

        def start(self, src):
            self.send(0, s, 0, on_x(1), src)
            self.send(2, s, 1, on_x(-1), src)
            self.send(1, s, 1, on_x(1), src)
            self.send(3, s, 0, on_x(-1), src)
            self.send(4, s, None, sib, src)

        def relay(self):
            self.arrived(0, on_x(-1), 0)
            self.send(5, on_x(-1), 0, on_x(1))
            self.arrived(2, on_x(1), 1)
            self.send(6, on_x(1), 1, on_x(-1))
            self.arrived(1, on_x(-1), 1)
            self.send(7, on_x(-1), None, sib)
            self.arrived(3, on_x(1), 0)
            self.send(8, on_x(1), None, sib)

        def finish(self):
            self.arrived(5, on_x(2), 0)
            self.arrived(6, on_x(2), 1)
            self.send(9, on_x(2), None, sib)
            self.arrived(4, sib, None)
            for k, dx in ((7, -1), (8, 1), (9, 2)):
                self.arrived(k, on_x(dx) + 1 - 2 * c, None)

    class Ring:
        def __init__(self, get, bufs, right, left):
            self.get, self.bufs, self.right, self.left = get, bufs, right, left
            self.ss, self.rs = sems.take(6), sems.take(6)

        def copy(self, k):
            source, landing, to = (
                (0, 2, self.right), (1, 3, self.left), (4, 8, self.right), (5, 9, self.right),
                (6, 10, self.left), (7, 11, self.left))[k]
            return remote(
                self.bufs.at[source], self.bufs.at[landing], self.ss(k), self.rs(k), *to)

        def send(self, k, value):
            self.bufs[(0, 1, 4, 5, 6, 7)[k]] = value.astype(BF)
            cp = self.copy(k)
            cp.start()
            pending.append(cp)

        def far(self):
            self.send(0, self.get(2, 0))
            self.send(1, self.get(2, 1))

        def to_right(self):
            self.send(3, self.get(1, 1))

        def to_left(self):
            self.send(4, self.get(3, 0))

        def start(self):
            self.far()
            self.to_right()
            self.to_left()

        def relay(self):
            self.copy(0).wait_recv()
            self.send(2, self.get(1, 0) + self.bufs[2].astype(F32))
            self.copy(1).wait_recv()
            self.send(5, self.get(3, 1) + self.bufs[3].astype(F32))

        def wait(self):
            for k in (3, 4, 2, 5):
                self.copy(k).wait_recv()

        def result(self, half):
            return (self.get(0, half) + self.bufs[8 + half].astype(F32)
                    + self.bufs[10 + half].astype(F32))

    class Scatter:
        def __init__(self, compute, keep, ssend, srecv, bufs):
            self.compute, self.keep, self.ssend, self.srecv = compute, keep, ssend, srecv
            self.s1, self.r1 = sems.take(4), sems.take(4)
            half = keep.shape[1] // 2
            self.ring = Ring(
                lambda k, h: keep[k, h * half:(h + 1) * half, :], bufs, (d, on_x(1)), (d, on_x(-1)))

        def to_sib(self, dx):
            return remote(self.ssend.at[dx], self.srecv.at[dx], self.s1(dx), self.r1(dx), d, sib)

        def start(self):
            for dx in (2, 1, 3, 0):
                self.ssend[dx] = self.compute((x + dx) % NX * 2 + 1 - c).astype(BF)
                cp = self.to_sib(dx)
                cp.start()
                pending.append(cp)

        def fill(self, dx):
            mine = self.compute((x + dx) % NX * 2 + c)
            self.to_sib(dx).wait_recv()
            self.keep[dx] = mine + self.srecv[dx].astype(F32)

        def middle(self):
            self.fill(2)
            self.ring.far()
            self.fill(1)
            self.ring.to_right()
            self.fill(3)
            self.ring.to_left()
            self.fill(0)

        def relay(self):
            self.ring.relay()

        def finish(self):
            self.ring.wait()
            return jnp.concatenate([self.ring.result(0), self.ring.result(1)], axis=0)

    class Swap:
        def __init__(self, src, dst):
            self.src, self.dst = src, dst
            self.ss, self.rs = sems.take(NJ), sems.take(NJ)

        def start(self):
            for j in range(NJ):
                peer = t_mine + S * j
                land = pl.multiple_of((d % S) * SLAB + (d // S) * GH, GH)
                cp = remote(
                    self.src.at[pl.ds(j * GH, GH), :], self.dst.at[pl.ds(land, GH), :],
                    self.ss(j), self.rs(d // S), peer, s)
                pl.when(peer != d)(cp.start)

                @pl.when(peer == d)
                def _():
                    self.dst[pl.ds(land, GH), :] = self.src[pl.ds(j * GH, GH), :]

        def finish(self):
            for j in range(NJ):
                peer = t_mine + S * j
                land = pl.multiple_of(t_mine * SLAB + j * GH, GH)
                cp = remote(
                    self.src.at[pl.ds(j * GH, GH), :], self.dst.at[pl.ds(land, GH), :],
                    self.ss(j), self.rs(j), peer, s)

                @pl.when(peer != d)
                def _():
                    cp.wait_recv()
                    cp.wait_send()

    gather_nodes = Gather(tbl, lambda q: q * N, N)
    gather_nodes.start(nodes_in)

    def permuted(values):
        ghost = values - PN
        part = ghost // GH
        place = PN + (part % S) * SLAB + (part // S) * GH + ghost % GH
        return jnp.where(values >= PN, place, values)

    def column(row):
        size = row.shape[1]
        hit = lax.broadcasted_iota(jnp.int32, (size, size), 0) == lax.broadcasted_iota(
            jnp.int32, (size, size), 1)
        return jnp.sum(jnp.where(hit, row.astype(F32), 0.0), axis=1, keepdims=True).astype(jnp.int32)

    def hot(mask):
        return jnp.where(mask, 1.0, 0.0).astype(BF)

    send_r = permuted(snd_row[...])
    recv_r = rcv_row[...]
    send_c = column(send_r)
    recv_c = column(recv_r)

    def build_t(r0):
        ids = lax.broadcasted_iota(jnp.int32, (256, E), 0) + r0
        pst[pl.ds(r0, 256), :] = hot(ids == send_r)

    rows_loop(PN + S * SLAB, 256, build_t)

    def build_rt(r0):
        ids = lax.broadcasted_iota(jnp.int32, (256, E), 0) + r0
        prt[pl.ds(r0, 256), :] = hot(ids == recv_r)

    rows_loop(PN, 256, build_rt)
    for c0 in range(0, PN + S * SLAB, 256):
        ids = lax.broadcasted_iota(jnp.int32, (E, 256), 1) + c0
        ps[:, c0:c0 + 256] = hot(ids == send_c)
        if c0 < PN:
            pr[:, c0:c0 + 256] = hot(ids == recv_c)

    lists = snd_lists[0]
    slot = lax.broadcasted_iota(jnp.int32, (S * SLAB, DOM), 0)
    part = slot // SLAB + (slot // GH) % NJ * S
    rows = hot(lax.broadcasted_iota(jnp.int32, (S * SLAB, DOM), 1) == part)
    high = dot(rows, (lists // 32).astype(F32).astype(BF))
    low = dot(rows, (lists % 32).astype(F32).astype(BF))
    slot = lax.broadcasted_iota(jnp.int32, (S * SLAB, GH), 0)
    here = lax.broadcasted_iota(jnp.int32, (S * SLAB, GH), 1) == slot % GH
    lists_c = jnp.sum(
        jnp.where(here, high * 32.0 + low, 0.0), axis=1, keepdims=True).astype(jnp.int32)

    loads[0].wait()
    loads[1].wait()

    def edge_part(r0):
        pre[pl.ds(r0, 256), :] = dot(edges[pl.ds(r0, 256), :], ein[0])

    rows_loop(E, 256, edge_part)

    gather_nodes.relay()
    gather_nodes.finish()

    hit = jnp.zeros((SLAB, 1), jnp.int32)
    for t in range(S):
        hit = jnp.where(t_mine == t, lists_c[t * SLAB:(t + 1) * SLAB, :], hit)
    pick = hot(lax.broadcasted_iota(jnp.int32, (SLAB, PN), 1) == hit)
    gsend[...] = dot(pick, tbl[:PN, :]).astype(BF)
    ghosts = tbl.at[pl.ds(PN, S * SLAB), :]
    swap_ghost = Swap(gsend, ghosts)
    swap_ghost.start()

    def gather_recv(r0):
        rows = pl.ds(r0, 256)
        got = dot(pr[rows, :], tbl[:PN, :]).astype(BF)
        recv[rows, :] = got
        pre[rows, :] = pre[rows, :] + dot(got, ein[2])

    rows_loop(E, 256, gather_recv)
    swap_ghost.finish()
    gather_ghost = Gather(ghosts, lambda q: ((q - d + DOM) % S) * SLAB, SLAB)
    gather_ghost.start(ghosts.at[pl.ds(pl.multiple_of(t_mine * SLAB, SLAB), SLAB), :])

    def gather_sent(r0):
        rows = pl.ds(r0, 256)
        sent_acc[rows, :] = dot(ps[rows, :PN], tbl[:PN, :])

    rows_loop(E, 256, gather_sent)
    gather_ghost.relay()
    gather_ghost.finish()

    loads[2].wait()
    edge_gain = egain[...]

    def edge_forward(r0):
        rows = pl.ds(r0, 256)
        got = (sent_acc[rows, :] + dot(ps[rows, PN:], tbl[PN:, :])).astype(BF)
        sent[rows, :] = got
        act = pre[rows, :] + dot(got, ein[1])
        pre[rows, :] = act
        hidden = swish(act).astype(BF)
        hid[rows, :] = hidden
        message = dot(hidden, eout[...])
        msg[rows, :] = message
        edges_out[rows, :] = (edges[rows, :].astype(F32) + normalize(message, edge_gain)).astype(BF)

    rows_loop(E, 256, edge_forward)

    def agg_block(q):
        return dot(prt[pl.ds(pl.multiple_of(q * N, N), N), :], edges_out[...])

    reduce_agg = Scatter(agg_block, agg_keep, aggs_send, aggs_recv, agg_bufs)
    reduce_agg.start()
    reduce_agg.middle()
    loads[3].wait()
    loads[4].wait()
    loads[5].wait()
    reduce_agg.relay()
    npre[...] = dot(nodes_in[...], nin[0])
    agg[...] = reduce_agg.finish().astype(BF)

    node_gain = ngain[...]
    act = npre[...] + dot(agg[...], nin[1])
    hidden = swish(act).astype(BF)
    nhid[...] = hidden
    message = dot(hidden, nout[...])
    nodes_out[...] = (nodes_in[...].astype(F32) + normalize(message, node_gain)).astype(BF)
    upstream = ncot[...].astype(F32)
    grad_message = normalize_back(message, node_gain, upstream).astype(BF)
    dnmsg[...] = grad_message
    grad_pre = (dot_nt(grad_message, nout[...]) * swish_slope(act)).astype(BF)
    dnpre[...] = grad_pre
    dagg_own[...] = dot_nt(grad_pre, nin[1]).astype(BF)
    dagg[pl.ds(pl.multiple_of(s * N, N), N), :] = dagg_own[...]

    gather_dagg = Gather(dagg, lambda q: q * N, N)
    gather_dagg.start(dagg_own)
    gdirect[...] = upstream + dot_nt(grad_pre, nin[0])

    mine_cols = pl.ds(pl.multiple_of(c * HALF, HALF), HALF)
    sib_cols = pl.ds(pl.multiple_of((1 - c) * HALF, HALF), HALF)

    class Weights:
        def __init__(self, base, pairs, ssend, srecv, own, ybufs, ysum, xbufs, zsend, zrecv):
            self.base, self.pairs, self.count = base, pairs, len(pairs)
            self.ssend, self.srecv, self.own, self.ysum = ssend, srecv, own, ysum
            self.zsend, self.zrecv = zsend, zrecv
            self.s0, self.r0 = sems.take(self.count), sems.take(self.count)
            self.sz, self.rz = sems.take(NZ - 1), sems.take(NZ - 1)

            def y_term(k, half):
                rows = pl.ds(pl.multiple_of((y + k) % NY * 128 + half * 64, 64), 64)
                return own[:, rows, :] + srecv[:, rows, :].astype(F32)

            def x_term(k, half):
                which = jnp.minimum((x + k) % NX, self.count - 1)
                return ysum[which, half * 64:(half + 1) * 64, :]

            self.y = Ring(
                y_term, ybufs, ((y + 1) % NY * NZ + z, s), ((y + NY - 1) % NY * NZ + z, s))
            self.x = Ring(x_term, xbufs, (d, on_x(1)), (d, on_x(-1)))

        def sib_copy(self, i):
            return remote(self.ssend.at[i], self.srecv.at[i], self.s0(i), self.r0(i), d, sib)

        def z_copy(self, k):
            return remote(
                self.zsend.at[k], self.zrecv.at[k - 1], self.sz(k - 1), self.rz(k - 1),
                y * NZ + (z + k) % NZ, s)

        def products(self, i):
            left, right = self.pairs[i]
            self.ssend[i] = dot_tn(left[...], right[:, sib_cols]).astype(BF)
            cp = self.sib_copy(i)
            cp.start()
            pending.append(cp)
            self.own[i] = dot_tn(left[...], right[:, mine_cols])

        def to_y(self):
            for i in range(self.count):
                self.sib_copy(i).wait_recv()
            self.y.start()

        def to_x(self):
            self.y.wait()
            for half in range(2):
                self.ysum[:, half * 64:(half + 1) * 64, :] = self.y.result(half)
            self.x.start()

        def to_z(self, total):
            self.x.wait()
            for half in range(2):
                total[half * 64:(half + 1) * 64, :] = self.x.result(half)
            for k in (4, 3, 5, 2, 6, 1, 7, 0):
                rows = pl.ds(pl.multiple_of((z + k) % NZ * 16, 16), 16)
                self.zsend[k] = total[rows, :].astype(BF)
                if k:
                    cp = self.z_copy(k)
                    cp.start()
                    pending.append(cp)

        def finish(self, out):
            for k in range(1, NZ):
                self.z_copy(k).wait_recv()
            total = self.zsend[0].astype(F32)
            for k in range(NZ - 1):
                total = total + self.zrecv[k].astype(F32)
            out[...] = total

    node_weights = Weights(
        4, ((nodes_in, dnpre), (agg, dnpre), (nhid, dnmsg)),
        fn_ssend, fn_srecv, fn_own, fn_ybufs, fn_ysum, fn_xbufs, fn_zsend, fn_zrecv)
    edge_weights = Weights(
        0, ((edges, dpre), (sent, dpre), (recv, dpre), (hid, dmsg)),
        fe_ssend, fe_srecv, fe_own, fe_ybufs, fe_ysum, fe_xbufs, fe_zsend, fe_zrecv)

    gather_dagg.relay()
    for i in range(3):
        node_weights.products(i)
    gather_dagg.finish()
    node_weights.to_y()

    def edge_backward(r0):
        rows = pl.ds(r0, 256)
        up = ecot[rows, :].astype(F32) + dot(pr[rows, :], dagg[...])
        gedge[rows, :] = up
        grad_msg = normalize_back(msg[rows, :], edge_gain, up).astype(BF)
        dmsg[rows, :] = grad_msg
        grad = (dot_nt(grad_msg, eout[...]) * swish_slope(pre[rows, :])).astype(BF)
        dpre[rows, :] = grad
        dsent[rows, :] = dot_nt(grad, ein[1]).astype(BF)

    rows_loop(E, 256, edge_backward)

    def ghost_block(q):
        place = PN + ((q - d + DOM) % S) * SLAB
        return dot(pst[pl.ds(pl.multiple_of(place, SLAB), SLAB), :], dsent[...])

    for i in (3, 0, 1, 2):
        edge_weights.products(i)
    node_weights.y.relay()
    reduce_ghost = Scatter(ghost_block, gg_keep, gg_ssend, gg_srecv, gg_bufs)
    reduce_ghost.start()
    edge_weights.to_y()
    reduce_ghost.middle()
    node_weights.to_x()

    def recv_grad(r0):
        rows = pl.ds(r0, 256)
        drecv[rows, :] = dot_nt(dpre[rows, :], ein[2]).astype(BF)

    rows_loop(E, 256, recv_grad)
    reduce_ghost.relay()

    def own_block(q):
        rows = pl.ds(pl.multiple_of(q * N, N), N)
        return dot(pst[rows, :], dsent[...]) + dot(prt[rows, :], drecv[...])

    reduce_own = Scatter(own_block, own_keep, own_ssend, own_srecv, own_bufs)
    reduce_own.start()
    edge_weights.y.relay()
    a2_send[...] = reduce_ghost.finish().astype(BF)
    swap_back = Swap(a2_send, retg)
    swap_back.start()
    reduce_own.middle()
    node_weights.x.relay()
    swap_back.finish()
    gather_back = Gather(retg, lambda q: ((q - d + DOM) % S) * SLAB, SLAB)
    gather_back.start(retg.at[pl.ds(pl.multiple_of(t_mine * SLAB, SLAB), SLAB), :])
    reduce_own.relay()
    edge_weights.to_x()
    gather_back.relay()
    node_weights.to_z(fz_total)

    def edge_grad(r0):
        rows = pl.ds(r0, 256)
        egrad[rows, :] = (gedge[rows, :] + dot_nt(dpre[rows, :], ein[0])).astype(BF)

    rows_loop(E, 256, edge_grad)
    edge_weights.x.relay()
    gather_back.finish()
    place = hot(lax.broadcasted_iota(jnp.int32, (S * SLAB, N), 1) + s * N == lists_c)
    direct = gdirect[...] + dot_tn(place, retg[...])
    edge_weights.to_z(fz_total)
    ngrad[...] = (direct + reduce_own.finish()).astype(BF)

    s_fin, r_fin = sems.take(6), sems.take(4)

    def fin_copy(group, i, slot, half):
        to = jnp.minimum(owner(group, i)[0], DOM * S - 1)
        return remote(
            fin.at[group], rows_in.at[slot, half], s_fin(3 * group + i), r_fin(2 * slot + half),
            to // S, to % S)

    def hand_out(group):
        for i in range(3):
            to, at, valid = owner(group, i)
            for slot in range(2):
                for half in range(2):
                    here = valid & (at == slot) & (c == half)
                    pl.when(here & (to != lin))(fin_copy(group, i, slot, half).start)

                    @pl.when(here & (to == lin))
                    def _():
                        rows_in[slot, half] = fin[group]

    node_weights.finish(fin.at[1])
    hand_out(1)
    edge_weights.finish(fin.at[0])
    hand_out(0)
    for slot in range(2):
        for half in range(2):
            pl.when(from_other(slot, half))(fin_copy(0, 0, slot, half).wait_recv)
    shift = first_row % 16
    for choice in range(0, 16, 2):
        @pl.when(shift == choice)
        def _():
            split = min(16 - choice, OUT_ROWS)
            for half in range(2):
                cols = slice(half * HALF, (half + 1) * HALF)
                wout[:split, cols] = rows_in[0, half, choice:choice + split, :]
                if split < OUT_ROWS:
                    wout[split:, cols] = rows_in[1, half, :OUT_ROWS - split, :]

    for cp in pending:
        cp.wait_send()
    for group in range(2):
        for i in range(3):
            to, _, valid = owner(group, i)
            pl.when(valid & (to != lin))(fin_copy(group, i, 0, 0).wait_send)


def scratch():
    def bf(*shape):
        return pltpu.VMEM(shape, BF)

    def f32(*shape):
        return pltpu.VMEM(shape, F32)

    T = PN + S * SLAB

    def scatter(rows):
        return [f32(NX, rows, D), bf(NX, rows, D), bf(NX, rows, D), bf(12, rows // 2, D)]

    def weights(count):
        return [
            bf(count, D, HALF), bf(count, D, HALF), f32(count, D, HALF),
            bf(12, count, 64, HALF), f32(count, 128, HALF), bf(12, 64, HALF),
            bf(NZ, 16, HALF), bf(NZ - 1, 16, HALF),
        ]

    return [
        bf(E, D), bf(3, D, D), bf(D, D), bf(2, D, D), bf(D, D), bf(E, D),
        bf(E, T), bf(E, PN), bf(T, E), bf(PN, E), bf(T, D), f32(E, D), bf(E, D), bf(E, D),
        f32(E, D), f32(E, D), bf(E, D),
        bf(SLAB, D), *scatter(N),
        bf(N, D), f32(N, D), bf(N, D), f32(N, D), bf(N, D), bf(N, D), bf(N, D), bf(PN, D),
        f32(E, D), bf(E, D), bf(E, D), bf(E, D), bf(E, D),
        *scatter(SLAB), bf(SLAB, D), bf(S * SLAB, D), *scatter(N),
        *weights(3), *weights(4),
        f32(128, HALF), f32(2, 16, HALF), f32(2, 2, 16, HALF),
        pltpu.SemaphoreType.DMA((N_SEM,)),
    ]


def hand_over(a0, a1, a2, a3, w_in, b0, b1, b2, b3, w_out):
    for src, dst in ((a0, b0), (a1, b1), (a2, b2), (a3, b3)):
        dst[...] = src[...]
    for i in range(OUT_ROWS):
        w_out[:, i * D:(i + 1) * D] = w_in[i:i + 1, :]


def body(
    node_state, edge_state, senders, receivers, send_rows, edge_in, edge_out, edge_gain,
    node_in, node_out, node_gain, node_cot, edge_cot,
):
    vmem = pl.BlockSpec(memory_space=pltpu.VMEM)
    hbm = pl.BlockSpec(memory_space=pl.ANY)
    states = (
        jax.ShapeDtypeStruct((N, D), BF),
        jax.ShapeDtypeStruct((E, D), BF),
        jax.ShapeDtypeStruct((N, D), BF),
        jax.ShapeDtypeStruct((E, D), BF),
    )
    results = pl.pallas_call(
        kernel,
        out_shape=states + (jax.ShapeDtypeStruct((OUT_ROWS, D), F32),),
        in_specs=[vmem] * 7 + [hbm] * 6,
        out_specs=[vmem] * 5,
        scratch_shapes=scratch(),
        compiler_params=pltpu.CompilerParams(
            collective_id=0, has_side_effects=True, vmem_limit_bytes=60 * 1024 * 1024),
    )(
        node_state, senders.reshape(1, E), receivers.reshape(1, E), send_rows,
        edge_gain, node_gain, node_cot,
        edge_state, edge_in[0], edge_out[0], node_in[0], node_out[0], edge_cot,
    )
    return pl.pallas_call(
        hand_over,
        out_shape=states + (jax.ShapeDtypeStruct((1, OUT_ROWS * D), F32),),
        in_specs=[vmem] * 5,
        out_specs=[vmem] * 5,
    )(*results)


def solution(mesh):
    both = P(("dom", "esplit"), None)
    in_specs = (
        both, both, P(("dom", "esplit")), P(("dom", "esplit")), P("dom", None, None),
        P(), P(), P(), P(), P(), P(), both, both,
    )
    out_specs = (both, both, both, both, P(None, ("dom", "esplit")))
    return jax.shard_map(body, mesh=mesh, in_specs=in_specs, out_specs=out_specs, check_vma=False)
```

time: 142 us -> 103 us (0.73)
  Pallas kernels: 139 us -> 100 us
    pallas_call x1, Pallas kernels: 42.2 us -> 2.34 us  [body(): pl.pallas_call(hand_over, out_shape=states + (jax.ShapeDtypeStruct((1, OU...]
where the time goes in v2:
time: 103 us; the launch traced here: 102 us
  Pallas kernels  100 us (97%)
  local copies, waits for them, and re-layouts  1.38 us (1%)
    pallas_call x1, Pallas kernels, body(): pl.pallas_call(kernel, out_shape=states + (jax.ShapeDtypeStruct((OUT_ROWS...  97.8 us
    pallas_call x1, Pallas kernels, body(): pl.pallas_call(hand_over, out_shape=states + (jax.ShapeDtypeStruct((1, OU...  2.34 us

profile of v2, /device:TPU:14, one launch (start us, length us, event | category | flops | bytes accessed | tf_op | source)
XLA Modules:
  0.0 102.2 jit_solution(17242877211502113331)
XLA Ops:
  0.6 1.4 %copy.18.snd_lists = s32[1,32,16]{2,1,0:T(8,128)} copy(s32[1,32,16]{1,2,0:T(8,128)} %param.17) | data formatting | bytes 4096 | tf_op args[4]
  2.0 97.8 %shard_map.164 = (bf16[128,512]{1,0:T(8,128)(2,1)}, bf16[512,512]{1,0:T(8,128)(2,1)}, bf16[128,512]{1,0:T(8,128)(2,1)}, bf16[512,512]{1,0:T(8,128)(2,1)}, f32[14,512]{1,0:T(8,128)}) custom-call(bf16[128,512]{1,0:T(8,128)(2,1)} %nodes_in.1, s32[1,512]{1,0:T(1,128)} %bitcast.10, s32[1,512]{1,0:T(1,128)} %bitcast.11, s32[1,32,16]{2,1,0:T(8,128)} %copy.18.snd_lists, ...), custom_call_target="tpu_custom_call" | custom-call | tf_op jit(solution)/shard_map/pallas_call | solution.py:743
  99.8 2.3 %shard_map.165 = (bf16[128,512]{1,0:T(8,128)(2,1)}, bf16[512,512]{1,0:T(8,128)(2,1)}, bf16[128,512]{1,0:T(8,128)(2,1)}, bf16[512,512]{1,0:T(8,128)(2,1)}, f32[1,7168]{1,0:T(1,128)}) custom-call(bf16[128,512]{1,0:T(8,128)(2,1)} %get-tuple-element.10.a0, bf16[512,512]{1,0:T(8,128)(2,1)} %get-tuple-element.11.a1, bf16[128,512]{1,0:T(8,128)(2,1)} %get-tuple-element.12.a2, ...), custom_call_target="tpu_custom_call" | custom-call | tf_op jit(solution)/shard_map/pallas_call | solution.py:756

commit v3 on v2

--- a/solution.py
+++ b/solution.py
@@ -96,14 +96,15 @@
     nodes_out, edges_out, ngrad, egrad, wout,
     edges, ein, eout, nin, nout, ecot,
     ps, pr, pst, prt, tbl, sent_acc, sent, recv, pre, msg, hid,
-    gsend, agg_keep, aggs_send, aggs_recv, agg_bufs,
+    gsend, aggs_send, aggs_recv, aggx_send, aggx_recv, agg_own,
     agg, npre, nhid, gdirect, dnpre, dnmsg, dagg_own, dagg,
     gedge, dmsg, dpre, dsent, drecv,
-    gg_keep, gg_ssend, gg_srecv, gg_bufs, a2_send, retg,
-    own_keep, own_ssend, own_srecv, own_bufs,
-    fn_ssend, fn_srecv, fn_own, fn_ybufs, fn_ysum, fn_xbufs, fn_zsend, fn_zrecv,
-    fe_ssend, fe_srecv, fe_own, fe_ybufs, fe_ysum, fe_xbufs, fe_zsend, fe_zrecv,
-    fz_total, fin, rows_in,
+    gg_ssend, gg_srecv, gg_xsend, gg_xrecv, gg_own, a2_send, retg,
+    own_ssend, own_srecv, own_xsend, own_xrecv, own_own,
+    fn_ssend, fn_srecv, fn_own, fn_ysend, fn_yrecv, fn_ysum, fn_xsend, fn_xrecv, fn_xsum, fn_zsend, fn_zrecv,
+    fe_ssend, fe_srecv, fe_own, fe_ysend, fe_yrecv, fe_ysum, fe_xsend, fe_xrecv, fe_xsum, fe_zsend, fe_zrecv,
+    fo_ssend, fo_srecv, fo_own, fo_zsend, fo_zrecv, fo_zsum, fo_ysend, fo_yrecv, fo_xsend, fo_xrecv,
+    fin, rows_in,
     sem_ref,
 ):
     d = lax.axis_index("dom")
@@ -142,7 +143,8 @@
     b_last = (first_row + OUT_ROWS - 1) // 16
 
     def holder(b, half):
-        return b % DOM, (b // DOM) % NX * 2 + half
+        r = b % DOM
+        return jnp.where(b // DOM == 3, r % NY * NZ + r // NY, r), (b // DOM) % NX * 2 + half
 
     def from_other(slot, half):
         dom, split = holder(b_first + slot, half)
@@ -167,7 +169,7 @@
     tbl[pl.ds(pl.multiple_of(s * N, N), N), :] = nodes_in[...]
 
     def owner(group, i):
-        b = DOM * (x + NX * group) + d
+        b = DOM * (x + NX * group) + (d if group else jnp.where(x == 3, z * NY + y, d))
         to = (16 * b) // OUT_ROWS + i
         valid = to <= (16 * b + 15) // OUT_ROWS
         if group:
@@ -188,115 +190,53 @@
 
     class Gather:
         def __init__(self, buf, offset, rows):
-            self.buf, self.offset, self.rows, self.half = buf, offset, rows, rows // 2
-            self.ss, self.rs = sems.take(10), sems.take(10)
-
-        def part(self, split, half):
-            start = pl.multiple_of(self.offset(split), self.rows)
-            if half is None:
-                return self.buf.at[pl.ds(start, self.rows), :]
-            return self.buf.at[pl.ds(start + half * self.half, self.half), :]
-
-        def copy(self, k, origin, half, split, src=None):
-            there = self.part(origin, half)
-            if src is None:
-                here = there
-            elif half is None:
-                here = src
-            else:
-                here = src.at[pl.ds(half * self.half, self.half), :]
+            self.buf, self.offset, self.rows = buf, offset, rows
+            self.ss, self.rs = sems.take(7), sems.take(7)
+
+        def copy(self, k, origin, split, src=None):
+            there = self.buf.at[pl.ds(pl.multiple_of(self.offset(origin), self.rows), self.rows), :]
+            here = there if src is None else src
             return remote(here, there, self.ss(k), self.rs(k), d, split)
 
-        def send(self, k, origin, half, split, src=None):
-            cp = self.copy(k, origin, half, split, src)
+        def send(self, k, origin, split, src=None):
+            cp = self.copy(k, origin, split, src)
             cp.start()
             pending.append(cp)
 
-        def arrived(self, k, origin, half):
-            self.copy(k, origin, half, sib).wait_recv()
-
         def start(self, src):
-            self.send(0, s, 0, on_x(1), src)
-            self.send(2, s, 1, on_x(-1), src)
-            self.send(1, s, 1, on_x(1), src)
-            self.send(3, s, 0, on_x(-1), src)
-            self.send(4, s, None, sib, src)
+            for dx in (2, 1, 3):
+                self.send(dx - 1, s, on_x(dx), src)
+            self.send(3, s, sib, src)
+
+        def forward(self, dx):
+            origin = on_x(-dx)
+            self.copy(dx - 1, origin, sib).wait_recv()
+            self.send(3 + dx, origin, sib)
 
         def relay(self):
-            self.arrived(0, on_x(-1), 0)
-            self.send(5, on_x(-1), 0, on_x(1))
-            self.arrived(2, on_x(1), 1)
-            self.send(6, on_x(1), 1, on_x(-1))
-            self.arrived(1, on_x(-1), 1)
-            self.send(7, on_x(-1), None, sib)
-            self.arrived(3, on_x(1), 0)
-            self.send(8, on_x(1), None, sib)
+            self.forward(1)
+            self.forward(3)
 
         def finish(self):
-            self.arrived(5, on_x(2), 0)
-            self.arrived(6, on_x(2), 1)
-            self.send(9, on_x(2), None, sib)
-            self.arrived(4, sib, None)
-            for k, dx in ((7, -1), (8, 1), (9, 2)):
-                self.arrived(k, on_x(dx) + 1 - 2 * c, None)
-
-    class Ring:
-        def __init__(self, get, bufs, right, left):
-            self.get, self.bufs, self.right, self.left = get, bufs, right, left
-            self.ss, self.rs = sems.take(6), sems.take(6)
-
-        def copy(self, k):
-            source, landing, to = (
-                (0, 2, self.right), (1, 3, self.left), (4, 8, self.right), (5, 9, self.right),
-                (6, 10, self.left), (7, 11, self.left))[k]
-            return remote(
-                self.bufs.at[source], self.bufs.at[landing], self.ss(k), self.rs(k), *to)
-
-        def send(self, k, value):
-            self.bufs[(0, 1, 4, 5, 6, 7)[k]] = value.astype(BF)
-            cp = self.copy(k)
-            cp.start()
-            pending.append(cp)
-
-        def far(self):
-            self.send(0, self.get(2, 0))
-            self.send(1, self.get(2, 1))
-
-        def to_right(self):
-            self.send(3, self.get(1, 1))
-
-        def to_left(self):
-            self.send(4, self.get(3, 0))
-
-        def start(self):
-            self.far()
-            self.to_right()
-            self.to_left()
-
-        def relay(self):
-            self.copy(0).wait_recv()
-            self.send(2, self.get(1, 0) + self.bufs[2].astype(F32))
-            self.copy(1).wait_recv()
-            self.send(5, self.get(3, 1) + self.bufs[3].astype(F32))
-
-        def wait(self):
-            for k in (3, 4, 2, 5):
-                self.copy(k).wait_recv()
-
-        def result(self, half):
-            return (self.get(0, half) + self.bufs[8 + half].astype(F32)
-                    + self.bufs[10 + half].astype(F32))
+            self.forward(2)
+            self.copy(3, sib, sib).wait_recv()
+            for dx in (1, 3, 2):
+                self.copy(3 + dx, on_x(-dx) + 1 - 2 * c, sib).wait_recv()
 
     class Scatter:
-        def __init__(self, compute, keep, ssend, srecv, bufs):
-            self.compute, self.keep, self.ssend, self.srecv = compute, keep, ssend, srecv
+        def __init__(self, compute, own, ssend, srecv, xsend, xrecv):
+            self.compute, self.own = compute, own
+            self.ssend, self.srecv, self.xsend, self.xrecv = ssend, srecv, xsend, xrecv
             self.s1, self.r1 = sems.take(4), sems.take(4)
-            half = keep.shape[1] // 2
-            self.ring = Ring(
-                lambda k, h: keep[k, h * half:(h + 1) * half, :], bufs, (d, on_x(1)), (d, on_x(-1)))
+            self.s2, self.r2 = sems.take(3), sems.take(3)
 
         def to_sib(self, dx):
             return remote(self.ssend.at[dx], self.srecv.at[dx], self.s1(dx), self.r1(dx), d, sib)
+
+        def to_chip(self, dx):
+            return remote(
+                self.xsend.at[dx - 1], self.xrecv.at[dx - 1], self.s2(dx - 1), self.r2(dx - 1),
+                d, on_x(dx))
 
         def start(self):
             for dx in (2, 1, 3, 0):
@@ -305,26 +245,24 @@
                 cp.start()
                 pending.append(cp)
 
-        def fill(self, dx):
-            mine = self.compute((x + dx) % NX * 2 + c)
-            self.to_sib(dx).wait_recv()
-            self.keep[dx] = mine + self.srecv[dx].astype(F32)
-
         def middle(self):
-            self.fill(2)
-            self.ring.far()
-            self.fill(1)
-            self.ring.to_right()
-            self.fill(3)
-            self.ring.to_left()
-            self.fill(0)
-
-        def relay(self):
-            self.ring.relay()
+            for dx in (2, 1, 3):
+                mine = self.compute(on_x(dx))
+                self.to_sib(dx).wait_recv()
+                self.xsend[dx - 1] = (mine + self.srecv[dx].astype(F32)).astype(BF)
+                cp = self.to_chip(dx)
+                cp.start()
+                pending.append(cp)
+            mine = self.compute(s)
+            self.to_sib(0).wait_recv()
+            self.own[...] = mine + self.srecv[0].astype(F32)
 
         def finish(self):
-            self.ring.wait()
-            return jnp.concatenate([self.ring.result(0), self.ring.result(1)], axis=0)
+            total = self.own[...]
+            for dx in (1, 3, 2):
+                self.to_chip(dx).wait_recv()
+                total = total + self.xrecv[dx - 1].astype(F32)
+            return total
 
     class Swap:
         def __init__(self, src, dst):
@@ -401,8 +339,8 @@
     slot = lax.broadcasted_iota(jnp.int32, (S * SLAB, DOM), 0)
     part = slot // SLAB + (slot // GH) % NJ * S
     rows = hot(lax.broadcasted_iota(jnp.int32, (S * SLAB, DOM), 1) == part)
-    high = dot(rows, (lists // 32).astype(F32).astype(BF))
-    low = dot(rows, (lists % 32).astype(F32).astype(BF))
+    high = dot_nt(rows, (lists // 32).astype(F32).astype(BF))
+    low = dot_nt(rows, (lists % 32).astype(F32).astype(BF))
     slot = lax.broadcasted_iota(jnp.int32, (S * SLAB, GH), 0)
     here = lax.broadcasted_iota(jnp.int32, (S * SLAB, GH), 1) == slot % GH
     lists_c = jnp.sum(
@@ -467,13 +405,12 @@
     def agg_block(q):
         return dot(prt[pl.ds(pl.multiple_of(q * N, N), N), :], edges_out[...])
 
-    reduce_agg = Scatter(agg_block, agg_keep, aggs_send, aggs_recv, agg_bufs)
+    reduce_agg = Scatter(agg_block, agg_own, aggs_send, aggs_recv, aggx_send, aggx_recv)
     reduce_agg.start()
     reduce_agg.middle()
     loads[3].wait()
     loads[4].wait()
     loads[5].wait()
-    reduce_agg.relay()
     npre[...] = dot(nodes_in[...], nin[0])
     agg[...] = reduce_agg.finish().astype(BF)
 
@@ -498,33 +435,13 @@
     mine_cols = pl.ds(pl.multiple_of(c * HALF, HALF), HALF)
     sib_cols = pl.ds(pl.multiple_of((1 - c) * HALF, HALF), HALF)
 
-    class Weights:
-        def __init__(self, base, pairs, ssend, srecv, own, ybufs, ysum, xbufs, zsend, zrecv):
-            self.base, self.pairs, self.count = base, pairs, len(pairs)
-            self.ssend, self.srecv, self.own, self.ysum = ssend, srecv, own, ysum
-            self.zsend, self.zrecv = zsend, zrecv
-            self.s0, self.r0 = sems.take(self.count), sems.take(self.count)
-            self.sz, self.rz = sems.take(NZ - 1), sems.take(NZ - 1)
-
-            def y_term(k, half):
-                rows = pl.ds(pl.multiple_of((y + k) % NY * 128 + half * 64, 64), 64)
-                return own[:, rows, :] + srecv[:, rows, :].astype(F32)
-
-            def x_term(k, half):
-                which = jnp.minimum((x + k) % NX, self.count - 1)
-                return ysum[which, half * 64:(half + 1) * 64, :]
-
-            self.y = Ring(
-                y_term, ybufs, ((y + 1) % NY * NZ + z, s), ((y + NY - 1) % NY * NZ + z, s))
-            self.x = Ring(x_term, xbufs, (d, on_x(1)), (d, on_x(-1)))
+    class Products:
+        def __init__(self, pairs, ssend, srecv, own):
+            self.pairs, self.ssend, self.srecv, self.own = pairs, ssend, srecv, own
+            self.s0, self.r0 = sems.take(len(pairs)), sems.take(len(pairs))
 
         def sib_copy(self, i):
             return remote(self.ssend.at[i], self.srecv.at[i], self.s0(i), self.r0(i), d, sib)
-
-        def z_copy(self, k):
-            return remote(
-                self.zsend.at[k], self.zrecv.at[k - 1], self.sz(k - 1), self.rz(k - 1),
-                y * NZ + (z + k) % NZ, s)
 
         def products(self, i):
             left, right = self.pairs[i]
@@ -534,49 +451,149 @@
             pending.append(cp)
             self.own[i] = dot_tn(left[...], right[:, mine_cols])
 
+        def chip_sum(self, i, rows):
+            return self.own[i, rows, :] + self.srecv[i, rows, :].astype(F32)
+
+    class Peers:
+        def __init__(self, count, send, recv, to):
+            self.count, self.sbuf, self.rbuf, self.to = count, send, recv, to
+            self.ss, self.rs = sems.take(count - 1), sems.take(count - 1)
+
+        def copy(self, k):
+            return remote(
+                self.sbuf.at[k - 1], self.rbuf.at[k - 1], self.ss(k - 1), self.rs(k - 1),
+                *self.to(k))
+
+        def send(self, k, value):
+            self.sbuf[k - 1] = value.astype(BF)
+            cp = self.copy(k)
+            cp.start()
+            pending.append(cp)
+
+        def total(self, mine):
+            for k in range(1, self.count):
+                self.copy(k).wait_recv()
+                mine = mine + self.rbuf[k - 1].astype(F32)
+            return mine
+
+    def on_y(k):
+        return (y + k) % NY * NZ + z, s
+
+    def on_z(k):
+        return y * NZ + (z + k) % NZ, s
+
+    Z_ORDER = (4, 3, 5, 2, 6, 1, 7)
+
+    class Weights(Products):
+        def __init__(self, pairs, ssend, srecv, own, ysend, yrecv, ysum, xsend, xrecv, xsum, zsend, zrecv):
+            super().__init__(pairs, ssend, srecv, own)
+            self.y = [Peers(NY, ysend.at[i], yrecv.at[i], on_y) for i in range(3)]
+            self.ysum, self.xsend, self.xrecv, self.xsum = ysum, xsend, xrecv, xsum
+            self.sx, self.rx = sems.take(NX - 1), sems.take(NX - 1)
+            self.z = Peers(NZ, zsend, zrecv, on_z)
+
+        def to_y(self, i):
+            self.sib_copy(i).wait_recv()
+            for k in (2, 1, 3):
+                rows = pl.ds(pl.multiple_of((y + k) % NY * 128, 128), 128)
+                self.y[i].send(k, self.chip_sum(i, rows))
+
+        def x_copy(self, k):
+            return remote(
+                self.xsend.at[k - 1], self.xrecv.at[k - 1], self.sx(k - 1), self.rx(k - 1),
+                d, on_x(k))
+
+        def to_x(self):
+            rows = pl.ds(pl.multiple_of(y * 128, 128), 128)
+            for i in range(3):
+                self.ysum[i] = self.y[i].total(self.chip_sum(i, rows))
+            for k in (2, 1, 3):
+                @pl.when((x + k) % NX < 3)
+                def _():
+                    self.xsend[k - 1] = self.ysum[(x + k) % NX].astype(BF)
+                    self.x_copy(k).start()
+
+        def to_z(self):
+            self.xsum[...] = self.ysum[jnp.minimum(x, 2)]
+
+            @pl.when(x < 3)
+            def _():
+                total = self.xsum[...]
+                for k in (1, 3, 2):
+                    self.x_copy(k).wait_recv()
+                    total = total + self.xrecv[k - 1].astype(F32)
+                self.xsum[...] = total
+            for k in Z_ORDER:
+                rows = pl.ds(pl.multiple_of((z + k) % NZ * 16, 16), 16)
+                self.z.send(k, self.xsum[rows, :])
+
+        def finish(self):
+            return self.z.total(self.xsum[pl.ds(pl.multiple_of(z * 16, 16), 16), :])
+
+        def drain(self):
+            for k in (2, 1, 3):
+                pl.when((x + k) % NX < 3)(self.x_copy(k).wait_send)
+
+    class LastWeights(Products):
+        def __init__(self, pairs, ssend, srecv, own, zsend, zrecv, zsum, ysend, yrecv, xsend, xrecv):
+            super().__init__(pairs, ssend, srecv, own)
+            self.zsum, self.xsend, self.xrecv = zsum, xsend, xrecv
+            self.z = Peers(NZ, zsend, zrecv, on_z)
+            self.y = Peers(NY, ysend, yrecv, on_y)
+            self.sx, self.rx = sems.take(1), sems.take(3)
+
+        def to_z(self):
+            self.sib_copy(0).wait_recv()
+            for k in Z_ORDER:
+                rows = pl.ds(pl.multiple_of((z + k) % NZ * 64, 64), 64)
+                self.z.send(k, self.chip_sum(0, rows))
+
         def to_y(self):
-            for i in range(self.count):
-                self.sib_copy(i).wait_recv()
-            self.y.start()
+            rows = pl.ds(pl.multiple_of(z * 64, 64), 64)
+            self.zsum[...] = self.z.total(self.chip_sum(0, rows))
+            for k in (2, 1, 3):
+                rows = pl.ds(pl.multiple_of((y + k) % NY * 16, 16), 16)
+                self.y.send(k, self.zsum[rows, :])
+
+        def x_copy(self, k):
+            return remote(self.xsend, self.xrecv.at[k], self.sx(0), self.rx(k), d, 6 + c)
 
         def to_x(self):
-            self.y.wait()
-            for half in range(2):
-                self.ysum[:, half * 64:(half + 1) * 64, :] = self.y.result(half)
-            self.x.start()
-
-        def to_z(self, total):
-            self.x.wait()
-            for half in range(2):
-                total[half * 64:(half + 1) * 64, :] = self.x.result(half)
-            for k in (4, 3, 5, 2, 6, 1, 7, 0):
-                rows = pl.ds(pl.multiple_of((z + k) % NZ * 16, 16), 16)
-                self.zsend[k] = total[rows, :].astype(BF)
-                if k:
-                    cp = self.z_copy(k)
-                    cp.start()
-                    pending.append(cp)
-
-        def finish(self, out):
-            for k in range(1, NZ):
-                self.z_copy(k).wait_recv()
-            total = self.zsend[0].astype(F32)
-            for k in range(NZ - 1):
-                total = total + self.zrecv[k].astype(F32)
-            out[...] = total
+            total = self.y.total(self.zsum[pl.ds(pl.multiple_of(y * 16, 16), 16), :])
+            fin[0] = total
+            self.xsend[...] = total.astype(BF)
+            for k in range(3):
+                pl.when(x == k)(self.x_copy(k).start)
+
+        def finish(self):
+            total = fin[0]
+            for k in range(3):
+                self.x_copy(k).wait_recv()
+                total = total + self.xrecv[k].astype(F32)
+            return total
+
+        def drain(self):
+            pl.when(x < 3)(self.x_copy(0).wait_send)
 
     node_weights = Weights(
-        4, ((nodes_in, dnpre), (agg, dnpre), (nhid, dnmsg)),
-        fn_ssend, fn_srecv, fn_own, fn_ybufs, fn_ysum, fn_xbufs, fn_zsend, fn_zrecv)
+        ((nodes_in, dnpre), (agg, dnpre), (nhid, dnmsg)),
+        fn_ssend, fn_srecv, fn_own, fn_ysend, fn_yrecv, fn_ysum, fn_xsend, fn_xrecv, fn_xsum,
+        fn_zsend, fn_zrecv)
     edge_weights = Weights(
-        0, ((edges, dpre), (sent, dpre), (recv, dpre), (hid, dmsg)),
-        fe_ssend, fe_srecv, fe_own, fe_ybufs, fe_ysum, fe_xbufs, fe_zsend, fe_zrecv)
-
-    gather_dagg.relay()
+        ((edges, dpre), (sent, dpre), (recv, dpre)),
+        fe_ssend, fe_srecv, fe_own, fe_ysend, fe_yrecv, fe_ysum, fe_xsend, fe_xrecv, fe_xsum,
+        fe_zsend, fe_zrecv)
+    out_weights = LastWeights(
+        ((hid, dmsg),),
+        fo_ssend, fo_srecv, fo_own, fo_zsend, fo_zrecv, fo_zsum, fo_ysend, fo_yrecv, fo_xsend,
+        fo_xrecv)
+
     for i in range(3):
         node_weights.products(i)
+    for i in range(3):
+        node_weights.to_y(i)
+    gather_dagg.relay()
     gather_dagg.finish()
-    node_weights.to_y()
 
     def edge_backward(r0):
         rows = pl.ds(r0, 256)
@@ -586,7 +603,6 @@
         dmsg[rows, :] = grad_msg
         grad = (dot_nt(grad_msg, eout[...]) * swish_slope(pre[rows, :])).astype(BF)
         dpre[rows, :] = grad
-        dsent[rows, :] = dot_nt(grad, ein[1]).astype(BF)
 
     rows_loop(E, 256, edge_backward)
 
@@ -594,52 +610,59 @@
         place = PN + ((q - d + DOM) % S) * SLAB
         return dot(pst[pl.ds(pl.multiple_of(place, SLAB), SLAB), :], dsent[...])
 
-    for i in (3, 0, 1, 2):
-        edge_weights.products(i)
-    node_weights.y.relay()
-    reduce_ghost = Scatter(ghost_block, gg_keep, gg_ssend, gg_srecv, gg_bufs)
+    out_weights.products(0)
+    edge_weights.products(0)
+    out_weights.to_z()
+    edge_weights.products(1)
+    edge_weights.to_y(0)
+    edge_weights.products(2)
+    edge_weights.to_y(1)
+
+    def send_grad(r0):
+        rows = pl.ds(r0, 256)
+        dsent[rows, :] = dot_nt(dpre[rows, :], ein[1]).astype(BF)
+
+    rows_loop(E, 256, send_grad)
+    reduce_ghost = Scatter(ghost_block, gg_own, gg_ssend, gg_srecv, gg_xsend, gg_xrecv)
     reduce_ghost.start()
-    edge_weights.to_y()
+    edge_weights.to_y(2)
     reduce_ghost.middle()
-    node_weights.to_x()
 
     def recv_grad(r0):
         rows = pl.ds(r0, 256)
         drecv[rows, :] = dot_nt(dpre[rows, :], ein[2]).astype(BF)
 
     rows_loop(E, 256, recv_grad)
-    reduce_ghost.relay()
 
     def own_block(q):
         rows = pl.ds(pl.multiple_of(q * N, N), N)
         return dot(pst[rows, :], dsent[...]) + dot(prt[rows, :], drecv[...])
 
-    reduce_own = Scatter(own_block, own_keep, own_ssend, own_srecv, own_bufs)
+    reduce_own = Scatter(own_block, own_own, own_ssend, own_srecv, own_xsend, own_xrecv)
     reduce_own.start()
-    edge_weights.y.relay()
+    node_weights.to_x()
     a2_send[...] = reduce_ghost.finish().astype(BF)
     swap_back = Swap(a2_send, retg)
     swap_back.start()
     reduce_own.middle()
-    node_weights.x.relay()
+
+    def edge_grad(r0):
+        rows = pl.ds(r0, 256)
+        egrad[rows, :] = (gedge[rows, :] + dot_nt(dpre[rows, :], ein[0])).astype(BF)
+
+    rows_loop(E, 256, edge_grad)
+    place = hot(lax.broadcasted_iota(jnp.int32, (S * SLAB, N), 1) + s * N == lists_c)
     swap_back.finish()
     gather_back = Gather(retg, lambda q: ((q - d + DOM) % S) * SLAB, SLAB)
     gather_back.start(retg.at[pl.ds(pl.multiple_of(t_mine * SLAB, SLAB), SLAB), :])
-    reduce_own.relay()
+    out_weights.to_y()
     edge_weights.to_x()
+    node_weights.to_z()
     gather_back.relay()
-    node_weights.to_z(fz_total)
-
-    def edge_grad(r0):
-        rows = pl.ds(r0, 256)
-        egrad[rows, :] = (gedge[rows, :] + dot_nt(dpre[rows, :], ein[0])).astype(BF)
-
-    rows_loop(E, 256, edge_grad)
-    edge_weights.x.relay()
+    out_weights.to_x()
     gather_back.finish()
-    place = hot(lax.broadcasted_iota(jnp.int32, (S * SLAB, N), 1) + s * N == lists_c)
+    edge_weights.to_z()
     direct = gdirect[...] + dot_tn(place, retg[...])
-    edge_weights.to_z(fz_total)
     ngrad[...] = (direct + reduce_own.finish()).astype(BF)
 
     s_fin, r_fin = sems.take(6), sems.take(4)
@@ -662,9 +685,18 @@
                     def _():
                         rows_in[slot, half] = fin[group]
 
-    node_weights.finish(fin.at[1])
+    fin[1] = node_weights.finish()
     hand_out(1)
-    edge_weights.finish(fin.at[0])
+    edge_block = edge_weights.finish()
+
+    @pl.when(x < 3)
+    def _():
+        fin[0] = edge_block
+
+    @pl.when(x == 3)
+    def _():
+        fin[0] = out_weights.finish()
+
     hand_out(0)
     for slot in range(2):
         for half in range(2):
@@ -682,6 +714,9 @@
 
     for cp in pending:
         cp.wait_send()
+    node_weights.drain()
+    edge_weights.drain()
+    out_weights.drain()
     for group in range(2):
         for i in range(3):
             to, _, valid = owner(group, i)
@@ -698,13 +733,16 @@
     T = PN + S * SLAB
 
     def scatter(rows):
-        return [f32(NX, rows, D), bf(NX, rows, D), bf(NX, rows, D), bf(12, rows // 2, D)]
-
-    def weights(count):
+        return [bf(NX, rows, D), bf(NX, rows, D), bf(NX - 1, rows, D), bf(NX - 1, rows, D), f32(rows, D)]
+
+    def products(count):
+        return [bf(count, D, HALF), bf(count, D, HALF), f32(count, D, HALF)]
+
+    def weights():
         return [
-            bf(count, D, HALF), bf(count, D, HALF), f32(count, D, HALF),
-            bf(12, count, 64, HALF), f32(count, 128, HALF), bf(12, 64, HALF),
-            bf(NZ, 16, HALF), bf(NZ - 1, 16, HALF),
+            *products(3), bf(3, NY - 1, 128, HALF), bf(3, NY - 1, 128, HALF), f32(3, 128, HALF),
+            bf(NX - 1, 128, HALF), bf(NX - 1, 128, HALF), f32(128, HALF),
+            bf(NZ - 1, 16, HALF), bf(NZ - 1, 16, HALF),
         ]
 
     return [
@@ -715,8 +753,10 @@
         bf(N, D), f32(N, D), bf(N, D), f32(N, D), bf(N, D), bf(N, D), bf(N, D), bf(PN, D),
         f32(E, D), bf(E, D), bf(E, D), bf(E, D), bf(E, D),
         *scatter(SLAB), bf(SLAB, D), bf(S * SLAB, D), *scatter(N),
-        *weights(3), *weights(4),
-        f32(128, HALF), f32(2, 16, HALF), f32(2, 2, 16, HALF),
+        *weights(), *weights(),
+        *products(1), bf(NZ - 1, 64, HALF), bf(NZ - 1, 64, HALF), f32(64, HALF),
+        bf(NY - 1, 16, HALF), bf(NY - 1, 16, HALF), bf(16, HALF), bf(NX - 1, 16, HALF),
+        f32(2, 16, HALF), f32(2, 2, 16, HALF),
         pltpu.SemaphoreType.DMA((N_SEM,)),
     ]
 
@@ -749,7 +789,8 @@
         compiler_params=pltpu.CompilerParams(
             collective_id=0, has_side_effects=True, vmem_limit_bytes=60 * 1024 * 1024),
     )(
-        node_state, senders.reshape(1, E), receivers.reshape(1, E), send_rows,
+        node_state, senders.reshape(1, E), receivers.reshape(1, E),
+        send_rows.transpose(0, 2, 1),
         edge_gain, node_gain, node_cot,
         edge_state, edge_in[0], edge_out[0], node_in[0], node_out[0], edge_cot,
     )

time: 103 us -> 98.5 us (0.956)
  Pallas kernels: 100 us -> 96.8 us
  local copies, waits for them, and re-layouts: 1.38 us -> 0 us
    pallas_call x1, Pallas kernels: 97.8 us -> 94.5 us  [body(): pl.pallas_call(kernel, out_shape=states + (jax.ShapeDtypeStruct((OUT_ROWS...]
    unnamed x1 -> x0, local copies, waits for them, and re-layouts: 1.38 us -> none
where the time goes in v3:
time: 98.5 us; the launch traced here: 97.5 us
  Pallas kernels  96.8 us (98%)
    pallas_call x1, Pallas kernels, body(): pl.pallas_call(kernel, out_shape=states + (jax.ShapeDtypeStruct((OUT_ROWS...  94.5 us
    pallas_call x1, Pallas kernels, body(): pl.pallas_call(hand_over, out_shape=states + (jax.ShapeDtypeStruct((1, OU...  2.34 us

profile of v3, /device:TPU:14, one launch (start us, length us, event | category | flops | bytes accessed | tf_op | source)
XLA Modules:
  0.0 97.5 jit_solution(7161736647432512503)
XLA Ops:
  0.6 94.5 %shard_map.164 = (bf16[128,512]{1,0:T(8,128)(2,1)}, bf16[512,512]{1,0:T(8,128)(2,1)}, bf16[128,512]{1,0:T(8,128)(2,1)}, bf16[512,512]{1,0:T(8,128)(2,1)}, f32[14,512]{1,0:T(8,128)}) custom-call(bf16[128,512]{1,0:T(8,128)(2,1)} %nodes_in.1, s32[1,512]{1,0:T(1,128)} %bitcast.12, s32[1,512]{1,0:T(1,128)} %bitcast.13, s32[1,16,32]{2,1,0:T(8,128)} %bitcast.11, ...), custom_call_target="tpu_custom_call" | custom-call | tf_op jit(solution)/shard_map/pallas_call | solution.py:783
  95.1 2.3 %shard_map.165 = (bf16[128,512]{1,0:T(8,128)(2,1)}, bf16[512,512]{1,0:T(8,128)(2,1)}, bf16[128,512]{1,0:T(8,128)(2,1)}, bf16[512,512]{1,0:T(8,128)(2,1)}, f32[1,7168]{1,0:T(1,128)}) custom-call(bf16[128,512]{1,0:T(8,128)(2,1)} %get-tuple-element.10.a0, bf16[512,512]{1,0:T(8,128)(2,1)} %get-tuple-element.11.a1, bf16[128,512]{1,0:T(8,128)(2,1)} %get-tuple-element.12.a2, ...), custom_call_target="tpu_custom_call" | custom-call | tf_op jit(solution)/shard_map/pallas_call | solution.py:797

commit v4 on v3

--- a/solution.py
+++ b/solution.py
@@ -87,23 +87,23 @@
         return lambda i: self.ref.at[base + i]
 
 
-N_SEM = 280
+N_SEM = 340
 
 
 def kernel(
     nodes_in, snd_row, rcv_row, snd_lists, egain, ngain, ncot,
     edges_hbm, ein_hbm, eout_hbm, nin_hbm, nout_hbm, ecot_hbm,
     nodes_out, edges_out, ngrad, egrad, wout,
-    edges, ein, eout, nin, nout, ecot,
+    nodes_out_v, edges_out_v, egrad_v, edges, ein, eout, nin, nout, ecot,
     ps, pr, pst, prt, tbl, sent_acc, sent, recv, pre, msg, hid,
     gsend, aggs_send, aggs_recv, aggx_send, aggx_recv, agg_own,
-    agg, npre, nhid, gdirect, dnpre, dnmsg, dagg_own, dagg,
+    agg, npre, nmsg, nhid, gdirect, dnpre, dnmsg, dagg_own, dagg,
     gedge, dmsg, dpre, dsent, drecv,
     gg_ssend, gg_srecv, gg_xsend, gg_xrecv, gg_own, a2_send, retg,
     own_ssend, own_srecv, own_xsend, own_xrecv, own_own,
-    fn_ssend, fn_srecv, fn_own, fn_ysend, fn_yrecv, fn_ysum, fn_xsend, fn_xrecv, fn_xsum, fn_zsend, fn_zrecv,
-    fe_ssend, fe_srecv, fe_own, fe_ysend, fe_yrecv, fe_ysum, fe_xsend, fe_xrecv, fe_xsum, fe_zsend, fe_zrecv,
-    fo_ssend, fo_srecv, fo_own, fo_zsend, fo_zrecv, fo_zsum, fo_ysend, fo_yrecv, fo_xsend, fo_xrecv,
+    fn_ssend, fn_srecv, fn_own, fn_ysend, fn_yrecv, fn_ysum, fn_zsend, fn_zrecv, fn_zsum, fn_xsend, fn_xrecv,
+    fe_ssend, fe_srecv, fe_own, fe_ysend, fe_yrecv, fe_ysum, fe_zsend, fe_zrecv, fe_zsum, fe_xsend, fe_xrecv,
+    fo_ssend, fo_srecv, fo_own, fo_zsend, fo_zrecv, fo_zsum, fo_ysend, fo_yrecv, fo_ysum, fo_xsend, fo_xrecv,
     fin, rows_in,
     sem_ref,
 ):
@@ -163,6 +163,12 @@
             ((edges_hbm, edges), (ein_hbm, ein), (eout_hbm, eout), (nin_hbm, nin),
              (nout_hbm, nout), (ecot_hbm, ecot)))
     ]
+    ssem = sems.take(3)
+    stores = [
+        pltpu.make_async_copy(a, b, ssem(i))
+        for i, (a, b) in enumerate(
+            ((edges_out_v, edges_out), (nodes_out_v, nodes_out), (egrad_v, egrad)))
+    ]
     for load in loads:
         load.start()
 
@@ -398,39 +404,59 @@
         hid[rows, :] = hidden
         message = dot(hidden, eout[...])
         msg[rows, :] = message
-        edges_out[rows, :] = (edges[rows, :].astype(F32) + normalize(message, edge_gain)).astype(BF)
+        edges_out_v[rows, :] = (edges[rows, :].astype(F32) + normalize(message, edge_gain)).astype(BF)
 
     rows_loop(E, 256, edge_forward)
 
-    def agg_block(q):
-        return dot(prt[pl.ds(pl.multiple_of(q * N, N), N), :], edges_out[...])
-
-    reduce_agg = Scatter(agg_block, agg_own, aggs_send, aggs_recv, aggx_send, aggx_recv)
-    reduce_agg.start()
-    reduce_agg.middle()
+    NH = N // 2
+
+    def agg_block(half):
+        def block(q):
+            return dot(prt[pl.ds(pl.multiple_of(q * N + half * NH, NH), NH), :], edges_out_v[...])
+
+        return block
+
+    reduce_agg = [
+        Scatter(agg_block(h), agg_own.at[h], aggs_send.at[h], aggs_recv.at[h], aggx_send.at[h],
+                aggx_recv.at[h])
+        for h in range(2)
+    ]
+    gather_dagg = [
+        Gather(dagg, functools.partial(lambda h, q: q * N + h * NH, h), NH) for h in range(2)
+    ]
+    for h in range(2):
+        reduce_agg[h].start()
+    for h in range(2):
+        reduce_agg[h].middle()
+    stores[0].start()
     loads[3].wait()
     loads[4].wait()
     loads[5].wait()
     npre[...] = dot(nodes_in[...], nin[0])
-    agg[...] = reduce_agg.finish().astype(BF)
-
     node_gain = ngain[...]
-    act = npre[...] + dot(agg[...], nin[1])
-    hidden = swish(act).astype(BF)
-    nhid[...] = hidden
-    message = dot(hidden, nout[...])
-    nodes_out[...] = (nodes_in[...].astype(F32) + normalize(message, node_gain)).astype(BF)
-    upstream = ncot[...].astype(F32)
-    grad_message = normalize_back(message, node_gain, upstream).astype(BF)
-    dnmsg[...] = grad_message
-    grad_pre = (dot_nt(grad_message, nout[...]) * swish_slope(act)).astype(BF)
-    dnpre[...] = grad_pre
-    dagg_own[...] = dot_nt(grad_pre, nin[1]).astype(BF)
-    dagg[pl.ds(pl.multiple_of(s * N, N), N), :] = dagg_own[...]
-
-    gather_dagg = Gather(dagg, lambda q: q * N, N)
-    gather_dagg.start(dagg_own)
-    gdirect[...] = upstream + dot_nt(grad_pre, nin[0])
+
+    for h in range(2):
+        rows = slice(h * NH, (h + 1) * NH)
+        sums = reduce_agg[h].finish().astype(BF)
+        agg[rows, :] = sums
+        act = npre[rows, :] + dot(sums, nin[1])
+        npre[rows, :] = act
+        hidden = swish(act).astype(BF)
+        nhid[rows, :] = hidden
+        message = dot(hidden, nout[...])
+        nmsg[rows, :] = message
+        upstream = ncot[rows, :].astype(F32)
+        grad_message = normalize_back(message, node_gain, upstream).astype(BF)
+        dnmsg[rows, :] = grad_message
+        grad_pre = (dot_nt(grad_message, nout[...]) * swish_slope(act)).astype(BF)
+        dnpre[rows, :] = grad_pre
+        dagg_own[rows, :] = dot_nt(grad_pre, nin[1]).astype(BF)
+        dagg[pl.ds(pl.multiple_of(s * N + h * NH, NH), NH), :] = dagg_own[rows, :]
+        gather_dagg[h].start(dagg_own.at[rows, :])
+    gdirect[...] = ncot[...].astype(F32) + dot_nt(dnpre[...], nin[0])
+    nodes_out_v[...] = (
+        nodes_in[...].astype(F32) + normalize(nmsg[...], node_gain)).astype(BF)
+    stores[1].start()
 
     mine_cols = pl.ds(pl.multiple_of(c * HALF, HALF), HALF)
     sib_cols = pl.ds(pl.multiple_of((1 - c) * HALF, HALF), HALF)
@@ -485,12 +511,12 @@
     Z_ORDER = (4, 3, 5, 2, 6, 1, 7)
 
     class Weights(Products):
-        def __init__(self, pairs, ssend, srecv, own, ysend, yrecv, ysum, xsend, xrecv, xsum, zsend, zrecv):
+        def __init__(self, pairs, ssend, srecv, own, ysend, yrecv, ysum, zsend, zrecv, zsum, xsend, xrecv):
             super().__init__(pairs, ssend, srecv, own)
             self.y = [Peers(NY, ysend.at[i], yrecv.at[i], on_y) for i in range(3)]
-            self.ysum, self.xsend, self.xrecv, self.xsum = ysum, xsend, xrecv, xsum
+            self.z = [Peers(NZ, zsend.at[i], zrecv.at[i], on_z) for i in range(3)]
+            self.ysum, self.zsum, self.xsend, self.xrecv = ysum, zsum, xsend, xrecv
             self.sx, self.rx = sems.take(NX - 1), sems.take(NX - 1)
-            self.z = Peers(NZ, zsend, zrecv, on_z)
 
         def to_y(self, i):
             self.sib_copy(i).wait_recv()
@@ -498,46 +524,43 @@
                 rows = pl.ds(pl.multiple_of((y + k) % NY * 128, 128), 128)
                 self.y[i].send(k, self.chip_sum(i, rows))
 
+        def to_z(self, i):
+            rows = pl.ds(pl.multiple_of(y * 128, 128), 128)
+            self.ysum[i] = self.y[i].total(self.chip_sum(i, rows))
+            for k in Z_ORDER:
+                rows = pl.ds(pl.multiple_of((z + k) % NZ * 16, 16), 16)
+                self.z[i].send(k, self.ysum[i, rows, :])
+
         def x_copy(self, k):
             return remote(
                 self.xsend.at[k - 1], self.xrecv.at[k - 1], self.sx(k - 1), self.rx(k - 1),
                 d, on_x(k))
 
         def to_x(self):
-            rows = pl.ds(pl.multiple_of(y * 128, 128), 128)
+            rows = pl.ds(pl.multiple_of(z * 16, 16), 16)
             for i in range(3):
-                self.ysum[i] = self.y[i].total(self.chip_sum(i, rows))
+                self.zsum[i] = self.z[i].total(self.ysum[i, rows, :])
             for k in (2, 1, 3):
                 @pl.when((x + k) % NX < 3)
                 def _():
-                    self.xsend[k - 1] = self.ysum[(x + k) % NX].astype(BF)
+                    self.xsend[k - 1] = self.zsum[(x + k) % NX].astype(BF)
                     self.x_copy(k).start()
 
-        def to_z(self):
-            self.xsum[...] = self.ysum[jnp.minimum(x, 2)]
-
-            @pl.when(x < 3)
-            def _():
-                total = self.xsum[...]
-                for k in (1, 3, 2):
-                    self.x_copy(k).wait_recv()
-                    total = total + self.xrecv[k - 1].astype(F32)
-                self.xsum[...] = total
-            for k in Z_ORDER:
-                rows = pl.ds(pl.multiple_of((z + k) % NZ * 16, 16), 16)
-                self.z.send(k, self.xsum[rows, :])
-
         def finish(self):
-            return self.z.total(self.xsum[pl.ds(pl.multiple_of(z * 16, 16), 16), :])
+            total = self.zsum[jnp.minimum(x, 2)]
+            for k in (1, 3, 2):
+                self.x_copy(k).wait_recv()
+                total = total + self.xrecv[k - 1].astype(F32)
+            return total
 
         def drain(self):
             for k in (2, 1, 3):
                 pl.when((x + k) % NX < 3)(self.x_copy(k).wait_send)
 
     class LastWeights(Products):
-        def __init__(self, pairs, ssend, srecv, own, zsend, zrecv, zsum, ysend, yrecv, xsend, xrecv):
+        def __init__(self, pairs, ssend, srecv, own, zsend, zrecv, zsum, ysend, yrecv, ysum, xsend, xrecv):
             super().__init__(pairs, ssend, srecv, own)
-            self.zsum, self.xsend, self.xrecv = zsum, xsend, xrecv
+            self.zsum, self.ysum, self.xsend, self.xrecv = zsum, ysum, xsend, xrecv
             self.z = Peers(NZ, zsend, zrecv, on_z)
             self.y = Peers(NY, ysend, yrecv, on_y)
             self.sx, self.rx = sems.take(1), sems.take(3)
@@ -560,13 +583,13 @@
 
         def to_x(self):
             total = self.y.total(self.zsum[pl.ds(pl.multiple_of(y * 16, 16), 16), :])
-            fin[0] = total
+            self.ysum[...] = total
             self.xsend[...] = total.astype(BF)
             for k in range(3):
                 pl.when(x == k)(self.x_copy(k).start)
 
         def finish(self):
-            total = fin[0]
+            total = self.ysum[...]
             for k in range(3):
                 self.x_copy(k).wait_recv()
                 total = total + self.xrecv[k].astype(F32)
@@ -577,23 +600,25 @@
 
     node_weights = Weights(
         ((nodes_in, dnpre), (agg, dnpre), (nhid, dnmsg)),
-        fn_ssend, fn_srecv, fn_own, fn_ysend, fn_yrecv, fn_ysum, fn_xsend, fn_xrecv, fn_xsum,
-        fn_zsend, fn_zrecv)
+        fn_ssend, fn_srecv, fn_own, fn_ysend, fn_yrecv, fn_ysum, fn_zsend, fn_zrecv, fn_zsum,
+        fn_xsend, fn_xrecv)
     edge_weights = Weights(
         ((edges, dpre), (sent, dpre), (recv, dpre)),
-        fe_ssend, fe_srecv, fe_own, fe_ysend, fe_yrecv, fe_ysum, fe_xsend, fe_xrecv, fe_xsum,
-        fe_zsend, fe_zrecv)
+        fe_ssend, fe_srecv, fe_own, fe_ysend, fe_yrecv, fe_ysum, fe_zsend, fe_zrecv, fe_zsum,
+        fe_xsend, fe_xrecv)
     out_weights = LastWeights(
         ((hid, dmsg),),
-        fo_ssend, fo_srecv, fo_own, fo_zsend, fo_zrecv, fo_zsum, fo_ysend, fo_yrecv, fo_xsend,
-        fo_xrecv)
+        fo_ssend, fo_srecv, fo_own, fo_zsend, fo_zrecv, fo_zsum, fo_ysend, fo_yrecv, fo_ysum,
+        fo_xsend, fo_xrecv)
 
     for i in range(3):
         node_weights.products(i)
     for i in range(3):
         node_weights.to_y(i)
-    gather_dagg.relay()
-    gather_dagg.finish()
+    for h in range(2):
+        gather_dagg[h].relay()
+    for h in range(2):
+        gather_dagg[h].finish()
 
     def edge_backward(r0):
         rows = pl.ds(r0, 256)
@@ -612,27 +637,27 @@
 
     out_weights.products(0)
     edge_weights.products(0)
-    out_weights.to_z()
-    edge_weights.products(1)
-    edge_weights.to_y(0)
-    edge_weights.products(2)
-    edge_weights.to_y(1)
 
     def send_grad(r0):
         rows = pl.ds(r0, 256)
         dsent[rows, :] = dot_nt(dpre[rows, :], ein[1]).astype(BF)
 
     rows_loop(E, 256, send_grad)
+    out_weights.to_z()
+    edge_weights.to_y(0)
     reduce_ghost = Scatter(ghost_block, gg_own, gg_ssend, gg_srecv, gg_xsend, gg_xrecv)
     reduce_ghost.start()
-    edge_weights.to_y(2)
+    edge_weights.products(1)
     reduce_ghost.middle()
+    edge_weights.to_y(1)
+    edge_weights.products(2)
 
     def recv_grad(r0):
         rows = pl.ds(r0, 256)
         drecv[rows, :] = dot_nt(dpre[rows, :], ein[2]).astype(BF)
 
     rows_loop(E, 256, recv_grad)
+    edge_weights.to_y(2)
 
     def own_block(q):
         rows = pl.ds(pl.multiple_of(q * N, N), N)
@@ -640,7 +665,8 @@
 
     reduce_own = Scatter(own_block, own_own, own_ssend, own_srecv, own_xsend, own_xrecv)
     reduce_own.start()
-    node_weights.to_x()
+    for i in range(3):
+        node_weights.to_z(i)
     a2_send[...] = reduce_ghost.finish().astype(BF)
     swap_back = Swap(a2_send, retg)
     swap_back.start()
@@ -648,21 +674,24 @@
 
     def edge_grad(r0):
         rows = pl.ds(r0, 256)
-        egrad[rows, :] = (gedge[rows, :] + dot_nt(dpre[rows, :], ein[0])).astype(BF)
+        egrad_v[rows, :] = (gedge[rows, :] + dot_nt(dpre[rows, :], ein[0])).astype(BF)
 
     rows_loop(E, 256, edge_grad)
+    stores[2].start()
     place = hot(lax.broadcasted_iota(jnp.int32, (S * SLAB, N), 1) + s * N == lists_c)
     swap_back.finish()
     gather_back = Gather(retg, lambda q: ((q - d + DOM) % S) * SLAB, SLAB)
     gather_back.start(retg.at[pl.ds(pl.multiple_of(t_mine * SLAB, SLAB), SLAB), :])
+    edge_weights.to_z(0)
     out_weights.to_y()
-    edge_weights.to_x()
-    node_weights.to_z()
+    node_weights.to_x()
+    edge_weights.to_z(1)
     gather_back.relay()
+    edge_weights.to_z(2)
     out_weights.to_x()
     gather_back.finish()
-    edge_weights.to_z()
     direct = gdirect[...] + dot_tn(place, retg[...])
+    edge_weights.to_x()
     ngrad[...] = (direct + reduce_own.finish()).astype(BF)
 
     s_fin, r_fin = sems.take(6), sems.take(4)
@@ -685,13 +714,15 @@
                     def _():
                         rows_in[slot, half] = fin[group]
 
-    fin[1] = node_weights.finish()
-    hand_out(1)
-    edge_block = edge_weights.finish()
-
     @pl.when(x < 3)
     def _():
-        fin[0] = edge_block
+        fin[1] = node_weights.finish()
+
+    hand_out(1)
+
+    @pl.when(x < 3)
+    def _():
+        fin[0] = edge_weights.finish()
 
     @pl.when(x == 3)
     def _():
@@ -712,6 +743,8 @@
                 if split < OUT_ROWS:
                     wout[split:, cols] = rows_in[1, half, :OUT_ROWS - split, :]
 
+    for store in stores:
+        store.wait()
     for cp in pending:
         cp.wait_send()
     node_weights.drain()
@@ -732,8 +765,11 @@
 
     T = PN + S * SLAB
 
-    def scatter(rows):
-        return [bf(NX, rows, D), bf(NX, rows, D), bf(NX - 1, rows, D), bf(NX - 1, rows, D), f32(rows, D)]
+    def scatter(rows, *lead):
+        return [
+            bf(*lead, NX, rows, D), bf(*lead, NX, rows, D), bf(*lead, NX - 1, rows, D),
+            bf(*lead, NX - 1, rows, D), f32(*lead, rows, D),
+        ]
 
     def products(count):
         return [bf(count, D, HALF), bf(count, D, HALF), f32(count, D, HALF)]
@@ -741,21 +777,22 @@
     def weights():
         return [
             *products(3), bf(3, NY - 1, 128, HALF), bf(3, NY - 1, 128, HALF), f32(3, 128, HALF),
-            bf(NX - 1, 128, HALF), bf(NX - 1, 128, HALF), f32(128, HALF),
-            bf(NZ - 1, 16, HALF), bf(NZ - 1, 16, HALF),
+            bf(3, NZ - 1, 16, HALF), bf(3, NZ - 1, 16, HALF), f32(3, 16, HALF),
+            bf(NX - 1, 16, HALF), bf(NX - 1, 16, HALF),
         ]
 
     return [
+        bf(N, D), bf(E, D), bf(E, D),
         bf(E, D), bf(3, D, D), bf(D, D), bf(2, D, D), bf(D, D), bf(E, D),
         bf(E, T), bf(E, PN), bf(T, E), bf(PN, E), bf(T, D), f32(E, D), bf(E, D), bf(E, D),
         f32(E, D), f32(E, D), bf(E, D),
-        bf(SLAB, D), *scatter(N),
-        bf(N, D), f32(N, D), bf(N, D), f32(N, D), bf(N, D), bf(N, D), bf(N, D), bf(PN, D),
+        bf(SLAB, D), *scatter(N // 2, 2),
+        bf(N, D), f32(N, D), f32(N, D), bf(N, D), f32(N, D), bf(N, D), bf(N, D), bf(N, D), bf(PN, D),
         f32(E, D), bf(E, D), bf(E, D), bf(E, D), bf(E, D),
         *scatter(SLAB), bf(SLAB, D), bf(S * SLAB, D), *scatter(N),
         *weights(), *weights(),
         *products(1), bf(NZ - 1, 64, HALF), bf(NZ - 1, 64, HALF), f32(64, HALF),
-        bf(NY - 1, 16, HALF), bf(NY - 1, 16, HALF), bf(16, HALF), bf(NX - 1, 16, HALF),
+        bf(NY - 1, 16, HALF), bf(NY - 1, 16, HALF), f32(16, HALF), bf(16, HALF), bf(NX - 1, 16, HALF),
         f32(2, 16, HALF), f32(2, 2, 16, HALF),
         pltpu.SemaphoreType.DMA((N_SEM,)),
     ]
@@ -784,7 +821,7 @@
         kernel,
         out_shape=states + (jax.ShapeDtypeStruct((OUT_ROWS, D), F32),),
         in_specs=[vmem] * 7 + [hbm] * 6,
-        out_specs=[vmem] * 5,
+        out_specs=[hbm, hbm, vmem, hbm, vmem],
         scratch_shapes=scratch(),
         compiler_params=pltpu.CompilerParams(
             collective_id=0, has_side_effects=True, vmem_limit_bytes=60 * 1024 * 1024),

time: 98.5 us -> 97.5 us (0.990)
  no operation moved by 1% of the time
where the time goes in v4:
time: 97.5 us; the launch traced here: 97.4 us
  Pallas kernels  96.8 us (99%)
    pallas_call x1, Pallas kernels, body(): pl.pallas_call(kernel, out_shape=states + (jax.ShapeDtypeStruct((OUT_ROWS...  94.4 us
    pallas_call x1, Pallas kernels, body(): pl.pallas_call(hand_over, out_shape=states + (jax.ShapeDtypeStruct((1, OU...  2.34 us

profile of v4, /device:TPU:14, one launch (start us, length us, event | category | flops | bytes accessed | tf_op | source)
XLA Modules:
  0.0 97.4 jit_solution(9650051059085500185)
XLA Ops:
  0.6 94.4 %shard_map.164 = (bf16[128,512]{1,0:T(8,128)(2,1)}, bf16[512,512]{1,0:T(8,128)(2,1)}, bf16[128,512]{1,0:T(8,128)(2,1)}, bf16[512,512]{1,0:T(8,128)(2,1)}, f32[14,512]{1,0:T(8,128)}) custom-call(bf16[128,512]{1,0:T(8,128)(2,1)} %nodes_in.1, s32[1,512]{1,0:T(1,128)} %bitcast.12, s32[1,512]{1,0:T(1,128)} %bitcast.13, s32[1,16,32]{2,1,0:T(8,128)} %bitcast.11, ...), custom_call_target="tpu_custom_call" | custom-call | tf_op jit(solution)/shard_map/pallas_call | solution.py:820
  95.1 2.3 %shard_map.165 = (bf16[128,512]{1,0:T(8,128)(2,1)}, bf16[512,512]{1,0:T(8,128)(2,1)}, bf16[128,512]{1,0:T(8,128)(2,1)}, bf16[512,512]{1,0:T(8,128)(2,1)}, f32[1,7168]{1,0:T(1,128)}) custom-call(bf16[128,512]{1,0:T(8,128)(2,1)} %get-tuple-element.10.a0, bf16[512,512]{1,0:T(8,128)(2,1)} %get-tuple-element.11.a1, bf16[128,512]{1,0:T(8,128)(2,1)} %get-tuple-element.12.a2, ...), custom_call_target="tpu_custom_call" | custom-call | tf_op jit(solution)/shard_map/pallas_call | solution.py:834

commit v5 on v4

--- a/solution.py
+++ b/solution.py
@@ -27,6 +27,7 @@
 HALF = D // 2
 NMAT = 7
 OUT_ROWS = 14
+BLOCK = 512
 
 
 def dot(a, b):
@@ -91,10 +92,10 @@
 
 
 def kernel(
-    nodes_in, snd_row, rcv_row, snd_lists, egain, ngain, ncot,
-    edges_hbm, ein_hbm, eout_hbm, nin_hbm, nout_hbm, ecot_hbm,
+    snd_row, rcv_row, snd_lists, egain, ngain,
+    nodes_hbm, ncot_hbm, edges_hbm, ein_hbm, eout_hbm, nin_hbm, nout_hbm, ecot_hbm,
     nodes_out, edges_out, ngrad, egrad, wout,
-    nodes_out_v, edges_out_v, egrad_v, edges, ein, eout, nin, nout, ecot,
+    nodes_in, ncot, nodes_out_v, edges_out_v, egrad_v, edges, ein, eout, nin, nout, ecot,
     ps, pr, pst, prt, tbl, sent_acc, sent, recv, pre, msg, hid,
     gsend, aggs_send, aggs_recv, aggx_send, aggx_recv, agg_own,
     agg, npre, nmsg, nhid, gdirect, dnpre, dnmsg, dagg_own, dagg,
@@ -156,12 +157,13 @@
             dom, split = holder(b_first + slot, half)
             pl.when(from_other(slot, half))(functools.partial(greet, dom, split))
 
-    lsem = sems.take(6)
+    lsem = sems.take(9)
     loads = [
         pltpu.make_async_copy(a, b, lsem(i))
         for i, (a, b) in enumerate(
             ((edges_hbm, edges), (ein_hbm, ein), (eout_hbm, eout), (nin_hbm, nin),
-             (nout_hbm, nout), (ecot_hbm, ecot)))
+             (nout_hbm, nout), (ecot_hbm, ecot), (nodes_hbm, nodes_in), (ncot_hbm, ncot),
+             (nodes_hbm, tbl.at[pl.ds(pl.multiple_of(s * N, N), N), :])))
     ]
     ssem = sems.take(3)
     stores = [
@@ -171,8 +173,6 @@
     ]
     for load in loads:
         load.start()
-
-    tbl[pl.ds(pl.multiple_of(s * N, N), N), :] = nodes_in[...]
 
     def owner(group, i):
         b = DOM * (x + NX * group) + (d if group else jnp.where(x == 3, z * NY + y, d))
@@ -302,7 +302,7 @@
                     cp.wait_send()
 
     gather_nodes = Gather(tbl, lambda q: q * N, N)
-    gather_nodes.start(nodes_in)
+    gather_nodes.start(nodes_hbm)
 
     def permuted(values):
         ghost = values - PN
@@ -356,10 +356,12 @@
     loads[1].wait()
 
     def edge_part(r0):
-        pre[pl.ds(r0, 256), :] = dot(edges[pl.ds(r0, 256), :], ein[0])
-
-    rows_loop(E, 256, edge_part)
-
+        rows = pl.ds(r0, BLOCK)
+        pre[rows, :] = dot(edges[rows, :], ein[0])
+
+    rows_loop(E, BLOCK, edge_part)
+
+    loads[8].wait()
     gather_nodes.relay()
     gather_nodes.finish()
 
@@ -373,21 +375,21 @@
     swap_ghost.start()
 
     def gather_recv(r0):
-        rows = pl.ds(r0, 256)
+        rows = pl.ds(r0, BLOCK)
         got = dot(pr[rows, :], tbl[:PN, :]).astype(BF)
         recv[rows, :] = got
         pre[rows, :] = pre[rows, :] + dot(got, ein[2])
 
-    rows_loop(E, 256, gather_recv)
+    rows_loop(E, BLOCK, gather_recv)
     swap_ghost.finish()
     gather_ghost = Gather(ghosts, lambda q: ((q - d + DOM) % S) * SLAB, SLAB)
     gather_ghost.start(ghosts.at[pl.ds(pl.multiple_of(t_mine * SLAB, SLAB), SLAB), :])
 
     def gather_sent(r0):
-        rows = pl.ds(r0, 256)
+        rows = pl.ds(r0, BLOCK)
         sent_acc[rows, :] = dot(ps[rows, :PN], tbl[:PN, :])
 
-    rows_loop(E, 256, gather_sent)
+    rows_loop(E, BLOCK, gather_sent)
     gather_ghost.relay()
     gather_ghost.finish()
 
@@ -395,7 +397,7 @@
     edge_gain = egain[...]
 
     def edge_forward(r0):
-        rows = pl.ds(r0, 256)
+        rows = pl.ds(r0, BLOCK)
         got = (sent_acc[rows, :] + dot(ps[rows, PN:], tbl[PN:, :])).astype(BF)
         sent[rows, :] = got
         act = pre[rows, :] + dot(got, ein[1])
@@ -406,7 +408,7 @@
         msg[rows, :] = message
         edges_out_v[rows, :] = (edges[rows, :].astype(F32) + normalize(message, edge_gain)).astype(BF)
 
-    rows_loop(E, 256, edge_forward)
+    rows_loop(E, BLOCK, edge_forward)
 
     NH = N // 2
 
@@ -432,6 +434,8 @@
     loads[3].wait()
     loads[4].wait()
     loads[5].wait()
+    loads[6].wait()
+    loads[7].wait()
     npre[...] = dot(nodes_in[...], nin[0])
     node_gain = ngain[...]
 
@@ -471,11 +475,13 @@
 
         def products(self, i):
             left, right = self.pairs[i]
-            self.ssend[i] = dot_tn(left[...], right[:, sib_cols]).astype(BF)
+            columns = jnp.concatenate([right[:, sib_cols], right[:, mine_cols]], axis=1)
+            grad = dot_tn(left[...], columns)
+            self.ssend[i] = grad[:, :HALF].astype(BF)
             cp = self.sib_copy(i)
             cp.start()
             pending.append(cp)
-            self.own[i] = dot_tn(left[...], right[:, mine_cols])
+            self.own[i] = grad[:, HALF:]
 
         def chip_sum(self, i, rows):
             return self.own[i, rows, :] + self.srecv[i, rows, :].astype(F32)
@@ -621,7 +627,7 @@
         gather_dagg[h].finish()
 
     def edge_backward(r0):
-        rows = pl.ds(r0, 256)
+        rows = pl.ds(r0, BLOCK)
         up = ecot[rows, :].astype(F32) + dot(pr[rows, :], dagg[...])
         gedge[rows, :] = up
         grad_msg = normalize_back(msg[rows, :], edge_gain, up).astype(BF)
@@ -629,7 +635,7 @@
         grad = (dot_nt(grad_msg, eout[...]) * swish_slope(pre[rows, :])).astype(BF)
         dpre[rows, :] = grad
 
-    rows_loop(E, 256, edge_backward)
+    rows_loop(E, BLOCK, edge_backward)
 
     def ghost_block(q):
         place = PN + ((q - d + DOM) % S) * SLAB
@@ -639,10 +645,10 @@
     edge_weights.products(0)
 
     def send_grad(r0):
-        rows = pl.ds(r0, 256)
+        rows = pl.ds(r0, BLOCK)
         dsent[rows, :] = dot_nt(dpre[rows, :], ein[1]).astype(BF)
 
-    rows_loop(E, 256, send_grad)
+    rows_loop(E, BLOCK, send_grad)
     out_weights.to_z()
     edge_weights.to_y(0)
     reduce_ghost = Scatter(ghost_block, gg_own, gg_ssend, gg_srecv, gg_xsend, gg_xrecv)
@@ -653,10 +659,10 @@
     edge_weights.products(2)
 
     def recv_grad(r0):
-        rows = pl.ds(r0, 256)
+        rows = pl.ds(r0, BLOCK)
         drecv[rows, :] = dot_nt(dpre[rows, :], ein[2]).astype(BF)
 
-    rows_loop(E, 256, recv_grad)
+    rows_loop(E, BLOCK, recv_grad)
     edge_weights.to_y(2)
 
     def own_block(q):
@@ -673,10 +679,10 @@
     reduce_own.middle()
 
     def edge_grad(r0):
-        rows = pl.ds(r0, 256)
+        rows = pl.ds(r0, BLOCK)
         egrad_v[rows, :] = (gedge[rows, :] + dot_nt(dpre[rows, :], ein[0])).astype(BF)
 
-    rows_loop(E, 256, edge_grad)
+    rows_loop(E, BLOCK, edge_grad)
     stores[2].start()
     place = hot(lax.broadcasted_iota(jnp.int32, (S * SLAB, N), 1) + s * N == lists_c)
     swap_back.finish()
@@ -686,12 +692,12 @@
     out_weights.to_y()
     node_weights.to_x()
     edge_weights.to_z(1)
+    edge_weights.to_z(2)
     gather_back.relay()
-    edge_weights.to_z(2)
     out_weights.to_x()
+    edge_weights.to_x()
     gather_back.finish()
     direct = gdirect[...] + dot_tn(place, retg[...])
-    edge_weights.to_x()
     ngrad[...] = (direct + reduce_own.finish()).astype(BF)
 
     s_fin, r_fin = sems.take(6), sems.take(4)
@@ -782,7 +788,7 @@
         ]
 
     return [
-        bf(N, D), bf(E, D), bf(E, D),
+        bf(N, D), bf(N, D), bf(N, D), bf(E, D), bf(E, D),
         bf(E, D), bf(3, D, D), bf(D, D), bf(2, D, D), bf(D, D), bf(E, D),
         bf(E, T), bf(E, PN), bf(T, E), bf(PN, E), bf(T, D), f32(E, D), bf(E, D), bf(E, D),
         f32(E, D), f32(E, D), bf(E, D),
@@ -820,16 +826,15 @@
     results = pl.pallas_call(
         kernel,
         out_shape=states + (jax.ShapeDtypeStruct((OUT_ROWS, D), F32),),
-        in_specs=[vmem] * 7 + [hbm] * 6,
+        in_specs=[vmem] * 5 + [hbm] * 8,
         out_specs=[hbm, hbm, vmem, hbm, vmem],
         scratch_shapes=scratch(),
         compiler_params=pltpu.CompilerParams(
             collective_id=0, has_side_effects=True, vmem_limit_bytes=60 * 1024 * 1024),
     )(
-        node_state, senders.reshape(1, E), receivers.reshape(1, E),
-        send_rows.transpose(0, 2, 1),
-        edge_gain, node_gain, node_cot,
-        edge_state, edge_in[0], edge_out[0], node_in[0], node_out[0], edge_cot,
+        senders.reshape(1, E), receivers.reshape(1, E), send_rows.transpose(0, 2, 1),
+        edge_gain, node_gain,
+        node_state, node_cot, edge_state, edge_in[0], edge_out[0], node_in[0], node_out[0], edge_cot,
     )
     return pl.pallas_call(
         hand_over,

time: 97.5 us -> 94 us (0.964)
  Pallas kernels: 96.8 us -> 93.2 us
    pallas_call x1, Pallas kernels: 94.4 us -> 90.9 us  [body(): pl.pallas_call(kernel, out_shape=states + (jax.ShapeDtypeStruct((OUT_ROWS...]
where the time goes in v5:
time: 94 us; the launch traced here: 93.9 us
  Pallas kernels  93.2 us (99%)
    pallas_call x1, Pallas kernels, body(): pl.pallas_call(kernel, out_shape=states + (jax.ShapeDtypeStruct((OUT_ROWS...  90.9 us
    pallas_call x1, Pallas kernels, body(): pl.pallas_call(hand_over, out_shape=states + (jax.ShapeDtypeStruct((1, OU...  2.34 us

profile of v5, /device:TPU:14, one launch (start us, length us, event | category | flops | bytes accessed | tf_op | source)
XLA Modules:
  0.0 93.9 jit_solution(11371046113481878865)
XLA Ops:
  0.6 90.9 %shard_map.164 = (bf16[128,512]{1,0:T(8,128)(2,1)}, bf16[512,512]{1,0:T(8,128)(2,1)}, bf16[128,512]{1,0:T(8,128)(2,1)}, bf16[512,512]{1,0:T(8,128)(2,1)}, f32[14,512]{1,0:T(8,128)}) custom-call(s32[1,512]{1,0:T(1,128)} %bitcast.12, s32[1,512]{1,0:T(1,128)} %bitcast.13, s32[1,16,32]{2,1,0:T(8,128)} %bitcast.11, f32[1,512]{1,0:T(1,128)} %egain.1, ...), custom_call_target="tpu_custom_call" | custom-call | tf_op jit(solution)/shard_map/pallas_call | solution.py:826
  91.5 2.3 %shard_map.165 = (bf16[128,512]{1,0:T(8,128)(2,1)}, bf16[512,512]{1,0:T(8,128)(2,1)}, bf16[128,512]{1,0:T(8,128)(2,1)}, bf16[512,512]{1,0:T(8,128)(2,1)}, f32[1,7168]{1,0:T(1,128)}) custom-call(bf16[128,512]{1,0:T(8,128)(2,1)} %get-tuple-element.10.a0, bf16[512,512]{1,0:T(8,128)(2,1)} %get-tuple-element.11.a1, bf16[128,512]{1,0:T(8,128)(2,1)} %get-tuple-element.12.a2, ...), custom_call_target="tpu_custom_call" | custom-call | tf_op jit(solution)/shard_map/pallas_call | solution.py:839

commit v6 on v5

--- a/solution.py
+++ b/solution.py
@@ -171,8 +171,6 @@
         for i, (a, b) in enumerate(
             ((edges_out_v, edges_out), (nodes_out_v, nodes_out), (egrad_v, egrad)))
     ]
-    for load in loads:
-        load.start()
 
     def owner(group, i):
         b = DOM * (x + NX * group) + (d if group else jnp.where(x == 3, z * NY + y, d))
@@ -223,11 +221,18 @@
             self.forward(1)
             self.forward(3)
 
+        def near(self):
+            self.copy(3, sib, sib).wait_recv()
+            for dx in (1, 3):
+                self.copy(3 + dx, on_x(-dx) + 1 - 2 * c, sib).wait_recv()
+
+        def far(self):
+            self.copy(5, on_x(2) + 1 - 2 * c, sib).wait_recv()
+
         def finish(self):
             self.forward(2)
-            self.copy(3, sib, sib).wait_recv()
-            for dx in (1, 3, 2):
-                self.copy(3 + dx, on_x(-dx) + 1 - 2 * c, sib).wait_recv()
+            self.near()
+            self.far()
 
     class Scatter:
         def __init__(self, compute, own, ssend, srecv, xsend, xrecv):
@@ -303,6 +308,8 @@
 
     gather_nodes = Gather(tbl, lambda q: q * N, N)
     gather_nodes.start(nodes_hbm)
+    for i in (8, 0, 1):
+        loads[i].start()
 
     def permuted(values):
         ghost = values - PN
@@ -364,6 +371,8 @@
     loads[8].wait()
     gather_nodes.relay()
     gather_nodes.finish()
+    for i in (2, 6, 3, 4, 7, 5):
+        loads[i].start()
 
     hit = jnp.zeros((SLAB, 1), jnp.int32)
     for t in range(S):
@@ -624,11 +633,23 @@
     for h in range(2):
         gather_dagg[h].relay()
     for h in range(2):
-        gather_dagg[h].finish()
+        gather_dagg[h].forward(2)
+    for h in range(2):
+        gather_dagg[h].near()
+
+    def chip_part(dx):
+        rows = pl.ds(pl.multiple_of((x + dx) % NX * 2 * N, 2 * N), 2 * N)
+        return dot(pr[:, rows], dagg[rows, :])
+
+    gedge[...] = ecot[...].astype(F32) + chip_part(0)
+    gedge[...] = gedge[...] + chip_part(1)
+    gedge[...] = gedge[...] + chip_part(3)
+    for h in range(2):
+        gather_dagg[h].far()
 
     def edge_backward(r0):
         rows = pl.ds(r0, BLOCK)
-        up = ecot[rows, :].astype(F32) + dot(pr[rows, :], dagg[...])
+        up = gedge[rows, :] + chip_part(2)
         gedge[rows, :] = up
         grad_msg = normalize_back(msg[rows, :], edge_gain, up).astype(BF)
         dmsg[rows, :] = grad_msg

time: 94 us -> 92.8 us (0.987)
  Pallas kernels: 93.2 us -> 92 us
    pallas_call x1, Pallas kernels: 90.9 us -> 89.6 us  [body(): pl.pallas_call(kernel, out_shape=states + (jax.ShapeDtypeStruct((OUT_ROWS...]
where the time goes in v6:
time: 92.8 us; the launch traced here: 92.6 us
  Pallas kernels  92 us (99%)
    pallas_call x1, Pallas kernels, body(): pl.pallas_call(kernel, out_shape=states + (jax.ShapeDtypeStruct((OUT_ROWS...  89.6 us
    pallas_call x1, Pallas kernels, body(): pl.pallas_call(hand_over, out_shape=states + (jax.ShapeDtypeStruct((1, OU...  2.34 us

profile of v6, /device:TPU:14, one launch (start us, length us, event | category | flops | bytes accessed | tf_op | source)
XLA Modules:
  0.0 92.6 jit_solution(6688575367044482568)
XLA Ops:
  0.6 89.6 %shard_map.164 = (bf16[128,512]{1,0:T(8,128)(2,1)}, bf16[512,512]{1,0:T(8,128)(2,1)}, bf16[128,512]{1,0:T(8,128)(2,1)}, bf16[512,512]{1,0:T(8,128)(2,1)}, f32[14,512]{1,0:T(8,128)}) custom-call(s32[1,512]{1,0:T(1,128)} %bitcast.12, s32[1,512]{1,0:T(1,128)} %bitcast.13, s32[1,16,32]{2,1,0:T(8,128)} %bitcast.11, f32[1,512]{1,0:T(1,128)} %egain.1, ...), custom_call_target="tpu_custom_call" | custom-call | tf_op jit(solution)/shard_map/pallas_call | solution.py:847
  90.3 2.3 %shard_map.165 = (bf16[128,512]{1,0:T(8,128)(2,1)}, bf16[512,512]{1,0:T(8,128)(2,1)}, bf16[128,512]{1,0:T(8,128)(2,1)}, bf16[512,512]{1,0:T(8,128)(2,1)}, f32[1,7168]{1,0:T(1,128)}) custom-call(bf16[128,512]{1,0:T(8,128)(2,1)} %get-tuple-element.10.a0, bf16[512,512]{1,0:T(8,128)(2,1)} %get-tuple-element.11.a1, bf16[128,512]{1,0:T(8,128)(2,1)} %get-tuple-element.12.a2, ...), custom_call_target="tpu_custom_call" | custom-call | tf_op jit(solution)/shard_map/pallas_call | solution.py:860

commit v7 on v6

--- a/solution.py
+++ b/solution.py
@@ -662,19 +662,19 @@
         place = PN + ((q - d + DOM) % S) * SLAB
         return dot(pst[pl.ds(pl.multiple_of(place, SLAB), SLAB), :], dsent[...])
 
+    edge_weights.products(0)
     out_weights.products(0)
-    edge_weights.products(0)
 
     def send_grad(r0):
         rows = pl.ds(r0, BLOCK)
         dsent[rows, :] = dot_nt(dpre[rows, :], ein[1]).astype(BF)
 
     rows_loop(E, BLOCK, send_grad)
-    out_weights.to_z()
-    edge_weights.to_y(0)
     reduce_ghost = Scatter(ghost_block, gg_own, gg_ssend, gg_srecv, gg_xsend, gg_xrecv)
     reduce_ghost.start()
+    edge_weights.to_y(0)
     edge_weights.products(1)
+    out_weights.to_z()
     reduce_ghost.middle()
     edge_weights.to_y(1)
     edge_weights.products(2)
@@ -714,13 +714,6 @@
     node_weights.to_x()
     edge_weights.to_z(1)
     edge_weights.to_z(2)
-    gather_back.relay()
-    out_weights.to_x()
-    edge_weights.to_x()
-    gather_back.finish()
-    direct = gdirect[...] + dot_tn(place, retg[...])
-    ngrad[...] = (direct + reduce_own.finish()).astype(BF)
-
     s_fin, r_fin = sems.take(6), sems.take(4)
 
     def fin_copy(group, i, slot, half):
@@ -741,11 +734,18 @@
                     def _():
                         rows_in[slot, half] = fin[group]
 
+    out_weights.to_x()
+    edge_weights.to_x()
+    gather_back.relay()
     @pl.when(x < 3)
     def _():
         fin[1] = node_weights.finish()
 
     hand_out(1)
+
+    gather_back.finish()
+    direct = gdirect[...] + dot_tn(place, retg[...])
+    ngrad[...] = (direct + reduce_own.finish()).astype(BF)
 
     @pl.when(x < 3)
     def _():
@@ -825,11 +825,29 @@
     ]
 
 
-def hand_over(a0, a1, a2, a3, w_in, b0, b1, b2, b3, w_out):
-    for src, dst in ((a0, b0), (a1, b1), (a2, b2), (a3, b3)):
-        dst[...] = src[...]
+def hand_over(a0, a1, a2, a3, w_in, b0, b1, b2, b3, w_out, v0, v1, v2, v3, sem_in, sem_out):
+    half = E // 2
+    pieces = []
+    for src, mid, dst in ((a1, v1, b1), (a3, v3, b3)):
+        for r0 in (0, half):
+            rows = pl.ds(r0, half)
+            pieces.append((src.at[rows, :], mid.at[rows, :], dst.at[rows, :]))
+    pieces += [(a0, v0, b0), (a2, v2, b2)]
+    loads = [
+        pltpu.make_async_copy(src, mid, sem_in.at[i]) for i, (src, mid, _) in enumerate(pieces)
+    ]
+    stores = [
+        pltpu.make_async_copy(mid, dst, sem_out.at[i]) for i, (_, mid, dst) in enumerate(pieces)
+    ]
+    for load in loads:
+        load.start()
     for i in range(OUT_ROWS):
         w_out[:, i * D:(i + 1) * D] = w_in[i:i + 1, :]
+    for load, store in zip(loads, stores):
+        load.wait()
+        store.start()
+    for store in stores:
+        store.wait()
 
 
 def body(
@@ -860,8 +878,10 @@
     return pl.pallas_call(
         hand_over,
         out_shape=states + (jax.ShapeDtypeStruct((1, OUT_ROWS * D), F32),),
-        in_specs=[vmem] * 5,
-        out_specs=[vmem] * 5,
+        in_specs=[hbm] * 4 + [vmem],
+        out_specs=[hbm] * 4 + [vmem],
+        scratch_shapes=[pltpu.VMEM(leaf.shape, BF) for leaf in states]
+        + [pltpu.SemaphoreType.DMA((6,)), pltpu.SemaphoreType.DMA((6,))],
     )(*results)
 
 

time: 92.8 us -> 94.8 us (1.022)
  Pallas kernels: 92 us -> 94 us
    pallas_call x1, Pallas kernels: 2.34 us -> 3.46 us  [body(): pl.pallas_call(hand_over, out_shape=states + (jax.ShapeDtypeStruct((1, OU...]
where the time goes in v7:
time: 94.8 us; the launch traced here: 94.6 us
  Pallas kernels  94 us (99%)
    pallas_call x1, Pallas kernels, body(): pl.pallas_call(kernel, out_shape=states + (jax.ShapeDtypeStruct((OUT_ROWS...  90.5 us
    pallas_call x1, Pallas kernels, body(): pl.pallas_call(hand_over, out_shape=states + (jax.ShapeDtypeStruct((1, OU...  3.46 us

profile of v7, /device:TPU:14, one launch (start us, length us, event | category | flops | bytes accessed | tf_op | source)
XLA Modules:
  0.0 94.6 jit_solution(7065111945591136709)
XLA Ops:
  0.6 90.5 %shard_map.164 = (bf16[128,512]{1,0:T(8,128)(2,1)}, bf16[512,512]{1,0:T(8,128)(2,1)}, bf16[128,512]{1,0:T(8,128)(2,1)}, bf16[512,512]{1,0:T(8,128)(2,1)}, f32[14,512]{1,0:T(8,128)}) custom-call(s32[1,512]{1,0:T(1,128)} %bitcast.12, s32[1,512]{1,0:T(1,128)} %bitcast.13, s32[1,16,32]{2,1,0:T(8,128)} %bitcast.11, f32[1,512]{1,0:T(1,128)} %egain.1, ...), custom_call_target="tpu_custom_call" | custom-call | tf_op jit(solution)/shard_map/pallas_call | solution.py:865
  91.2 3.5 %shard_map.165 = (bf16[128,512]{1,0:T(8,128)(2,1)}, bf16[512,512]{1,0:T(8,128)(2,1)}, bf16[128,512]{1,0:T(8,128)(2,1)}, bf16[512,512]{1,0:T(8,128)(2,1)}, f32[1,7168]{1,0:T(1,128)}) custom-call(bf16[128,512]{1,0:T(8,128)(2,1)} %get-tuple-element.10.a0, bf16[512,512]{1,0:T(8,128)(2,1)} %get-tuple-element.11.a1, bf16[128,512]{1,0:T(8,128)(2,1)} %get-tuple-element.12.a2, ...), custom_call_target="tpu_custom_call" | custom-call | tf_op jit(solution)/shard_map/pallas_call | solution.py:878

commit v8 on v6

--- a/solution.py
+++ b/solution.py
@@ -234,6 +234,9 @@
             self.near()
             self.far()
 
+    def target(near, dx):
+        return (x + dx) % NX * 2 + (c if near else 1 - c)
+
     class Scatter:
         def __init__(self, compute, own, ssend, srecv, xsend, xrecv):
             self.compute, self.own = compute, own
@@ -251,20 +254,20 @@
 
         def start(self):
             for dx in (2, 1, 3, 0):
-                self.ssend[dx] = self.compute((x + dx) % NX * 2 + 1 - c).astype(BF)
+                self.ssend[dx] = self.compute(0, dx).astype(BF)
                 cp = self.to_sib(dx)
                 cp.start()
                 pending.append(cp)
 
         def middle(self):
             for dx in (2, 1, 3):
-                mine = self.compute(on_x(dx))
+                mine = self.compute(1, dx)
                 self.to_sib(dx).wait_recv()
                 self.xsend[dx - 1] = (mine + self.srecv[dx].astype(F32)).astype(BF)
                 cp = self.to_chip(dx)
                 cp.start()
                 pending.append(cp)
-            mine = self.compute(s)
+            mine = self.compute(1, 0)
             self.to_sib(0).wait_recv()
             self.own[...] = mine + self.srecv[0].astype(F32)
 
@@ -337,11 +340,11 @@
 
     rows_loop(PN + S * SLAB, 256, build_t)
 
-    def build_rt(r0):
-        ids = lax.broadcasted_iota(jnp.int32, (256, E), 0) + r0
-        prt[pl.ds(r0, 256), :] = hot(ids == recv_r)
-
-    rows_loop(PN, 256, build_rt)
+    for near in range(2):
+        for dx in range(NX):
+            r0 = (near * NX + dx) * N
+            ids = lax.broadcasted_iota(jnp.int32, (N, E), 0) + target(near, dx) * N
+            prt[r0:r0 + N, :] = hot(ids == recv_r)
     for c0 in range(0, PN + S * SLAB, 256):
         ids = lax.broadcasted_iota(jnp.int32, (E, 256), 1) + c0
         ps[:, c0:c0 + 256] = hot(ids == send_c)
@@ -421,9 +424,13 @@
 
     NH = N // 2
 
+    agg_all = [None, None]
+
     def agg_block(half):
-        def block(q):
-            return dot(prt[pl.ds(pl.multiple_of(q * N + half * NH, NH), NH), :], edges_out_v[...])
+        def block(near, dx):
+            if agg_all[near] is None:
+                agg_all[near] = dot(prt[near * NX * N:(near + 1) * NX * N, :], edges_out_v[...])
+            return agg_all[near][dx * N + half * NH:dx * N + (half + 1) * NH, :]
 
         return block
 
@@ -658,23 +665,23 @@
 
     rows_loop(E, BLOCK, edge_backward)
 
-    def ghost_block(q):
-        place = PN + ((q - d + DOM) % S) * SLAB
+    def ghost_block(near, dx):
+        place = PN + ((target(near, dx) - d + DOM) % S) * SLAB
         return dot(pst[pl.ds(pl.multiple_of(place, SLAB), SLAB), :], dsent[...])
 
+    edge_weights.products(0)
     out_weights.products(0)
-    edge_weights.products(0)
 
     def send_grad(r0):
         rows = pl.ds(r0, BLOCK)
         dsent[rows, :] = dot_nt(dpre[rows, :], ein[1]).astype(BF)
 
     rows_loop(E, BLOCK, send_grad)
-    out_weights.to_z()
-    edge_weights.to_y(0)
     reduce_ghost = Scatter(ghost_block, gg_own, gg_ssend, gg_srecv, gg_xsend, gg_xrecv)
     reduce_ghost.start()
+    edge_weights.to_y(0)
     edge_weights.products(1)
+    out_weights.to_z()
     reduce_ghost.middle()
     edge_weights.to_y(1)
     edge_weights.products(2)
@@ -686,18 +693,19 @@
     rows_loop(E, BLOCK, recv_grad)
     edge_weights.to_y(2)
 
-    def own_block(q):
-        rows = pl.ds(pl.multiple_of(q * N, N), N)
-        return dot(pst[rows, :], dsent[...]) + dot(prt[rows, :], drecv[...])
+    def own_block(near, dx):
+        rows = pl.ds(pl.multiple_of(target(near, dx) * N, N), N)
+        r0 = (near * NX + dx) * N
+        return dot(pst[rows, :], dsent[...]) + dot(prt[r0:r0 + N, :], drecv[...])
 
     reduce_own = Scatter(own_block, own_own, own_ssend, own_srecv, own_xsend, own_xrecv)
     reduce_own.start()
-    for i in range(3):
-        node_weights.to_z(i)
+    reduce_own.middle()
     a2_send[...] = reduce_ghost.finish().astype(BF)
     swap_back = Swap(a2_send, retg)
     swap_back.start()
-    reduce_own.middle()
+    for i in range(3):
+        node_weights.to_z(i)
 
     def edge_grad(r0):
         rows = pl.ds(r0, BLOCK)
@@ -714,13 +722,6 @@
     node_weights.to_x()
     edge_weights.to_z(1)
     edge_weights.to_z(2)
-    gather_back.relay()
-    out_weights.to_x()
-    edge_weights.to_x()
-    gather_back.finish()
-    direct = gdirect[...] + dot_tn(place, retg[...])
-    ngrad[...] = (direct + reduce_own.finish()).astype(BF)
-
     s_fin, r_fin = sems.take(6), sems.take(4)
 
     def fin_copy(group, i, slot, half):
@@ -741,11 +742,18 @@
                     def _():
                         rows_in[slot, half] = fin[group]
 
+    out_weights.to_x()
+    edge_weights.to_x()
+    gather_back.relay()
     @pl.when(x < 3)
     def _():
         fin[1] = node_weights.finish()
 
     hand_out(1)
+
+    gather_back.finish()
+    direct = gdirect[...] + dot_tn(place, retg[...])
+    ngrad[...] = (direct + reduce_own.finish()).astype(BF)
 
     @pl.when(x < 3)
     def _():

time: 92.8 us -> 92.4 us (level)
  no operation moved by 1% of the time
where the time goes in v8:
time: 92.4 us; the launch traced here: 92.3 us
  Pallas kernels  91.6 us (99%)
    pallas_call x1, Pallas kernels, body(): pl.pallas_call(kernel, out_shape=states + (jax.ShapeDtypeStruct((OUT_ROWS...  89.3 us
    pallas_call x1, Pallas kernels, body(): pl.pallas_call(hand_over, out_shape=states + (jax.ShapeDtypeStruct((1, OU...  2.34 us

profile of v8, /device:TPU:14, one launch (start us, length us, event | category | flops | bytes accessed | tf_op | source)
XLA Modules:
  0.0 92.3 jit_solution(13397839695647128150)
XLA Ops:
  0.6 89.3 %shard_map.164 = (bf16[128,512]{1,0:T(8,128)(2,1)}, bf16[512,512]{1,0:T(8,128)(2,1)}, bf16[128,512]{1,0:T(8,128)(2,1)}, bf16[512,512]{1,0:T(8,128)(2,1)}, f32[14,512]{1,0:T(8,128)}) custom-call(s32[1,512]{1,0:T(1,128)} %bitcast.12, s32[1,512]{1,0:T(1,128)} %bitcast.13, s32[1,16,32]{2,1,0:T(8,128)} %bitcast.11, f32[1,512]{1,0:T(1,128)} %egain.1, ...), custom_call_target="tpu_custom_call" | custom-call | tf_op jit(solution)/shard_map/pallas_call | solution.py:855
  89.9 2.3 %shard_map.165 = (bf16[128,512]{1,0:T(8,128)(2,1)}, bf16[512,512]{1,0:T(8,128)(2,1)}, bf16[128,512]{1,0:T(8,128)(2,1)}, bf16[512,512]{1,0:T(8,128)(2,1)}, f32[1,7168]{1,0:T(1,128)}) custom-call(bf16[128,512]{1,0:T(8,128)(2,1)} %get-tuple-element.10.a0, bf16[512,512]{1,0:T(8,128)(2,1)} %get-tuple-element.11.a1, bf16[128,512]{1,0:T(8,128)(2,1)} %get-tuple-element.12.a2, ...), custom_call_target="tpu_custom_call" | custom-call | tf_op jit(solution)/shard_map/pallas_call | solution.py:868

commit v9 on v8

--- a/solution.py
+++ b/solution.py
@@ -669,8 +669,6 @@
         place = PN + ((target(near, dx) - d + DOM) % S) * SLAB
         return dot(pst[pl.ds(pl.multiple_of(place, SLAB), SLAB), :], dsent[...])
 
-    edge_weights.products(0)
-    out_weights.products(0)
 
     def send_grad(r0):
         rows = pl.ds(r0, BLOCK)
@@ -679,10 +677,12 @@
     rows_loop(E, BLOCK, send_grad)
     reduce_ghost = Scatter(ghost_block, gg_own, gg_ssend, gg_srecv, gg_xsend, gg_xrecv)
     reduce_ghost.start()
+    edge_weights.products(0)
+    out_weights.products(0)
+    reduce_ghost.middle()
     edge_weights.to_y(0)
     edge_weights.products(1)
     out_weights.to_z()
-    reduce_ghost.middle()
     edge_weights.to_y(1)
     edge_weights.products(2)
 

time: 92.4 us -> 93.1 us (level)
  no operation moved by 1% of the time
where the time goes in v9:
time: 93.1 us; the launch traced here: 92.7 us
  Pallas kernels  92.1 us (99%)
    pallas_call x1, Pallas kernels, body(): pl.pallas_call(kernel, out_shape=states + (jax.ShapeDtypeStruct((OUT_ROWS...  89.7 us
    pallas_call x1, Pallas kernels, body(): pl.pallas_call(hand_over, out_shape=states + (jax.ShapeDtypeStruct((1, OU...  2.34 us

profile of v9, /device:TPU:14, one launch (start us, length us, event | category | flops | bytes accessed | tf_op | source)
XLA Modules:
  0.0 92.7 jit_solution(5548705445466702514)
XLA Ops:
  0.6 89.7 %shard_map.164 = (bf16[128,512]{1,0:T(8,128)(2,1)}, bf16[512,512]{1,0:T(8,128)(2,1)}, bf16[128,512]{1,0:T(8,128)(2,1)}, bf16[512,512]{1,0:T(8,128)(2,1)}, f32[14,512]{1,0:T(8,128)}) custom-call(s32[1,512]{1,0:T(1,128)} %bitcast.12, s32[1,512]{1,0:T(1,128)} %bitcast.13, s32[1,16,32]{2,1,0:T(8,128)} %bitcast.11, f32[1,512]{1,0:T(1,128)} %egain.1, ...), custom_call_target="tpu_custom_call" | custom-call | tf_op jit(solution)/shard_map/pallas_call | solution.py:855
  90.4 2.3 %shard_map.165 = (bf16[128,512]{1,0:T(8,128)(2,1)}, bf16[512,512]{1,0:T(8,128)(2,1)}, bf16[128,512]{1,0:T(8,128)(2,1)}, bf16[512,512]{1,0:T(8,128)(2,1)}, f32[1,7168]{1,0:T(1,128)}) custom-call(bf16[128,512]{1,0:T(8,128)(2,1)} %get-tuple-element.10.a0, bf16[512,512]{1,0:T(8,128)(2,1)} %get-tuple-element.11.a1, bf16[128,512]{1,0:T(8,128)(2,1)} %get-tuple-element.12.a2, ...), custom_call_target="tpu_custom_call" | custom-call | tf_op jit(solution)/shard_map/pallas_call | solution.py:868
